TPU v7x, 512 devices: a whole 4x4x16 slice. The times are simulated.
512 devices in a mesh: gx: 16 (over x, z_lo), gy: 32 (over z_hi, y, core).
Axes of the slice: x: 4, y: 4, z: 16 (z_hi: 4, z_lo: 4; z = z_hi * 4 + z_lo), core: 2. Of those that a mesh axis runs over, the one named last changes fastest.
Arguments:
- object_slices: float32 [4, 2, 2048, 4096], P(None, None, 'gy', 'gx'), may hold values from -6 to 6
- probe: float32 [2, 128, 128], replicated, may hold values from -6 to 6
- positions: int32 [32, 16, 2, 2], P('gy', 'gx'), may hold values from 0 to 3968, as said below
- counts: int32 [32, 16], P('gy', 'gx'), may hold values from 1 to 2, as said below
- measured: float32 [32, 16, 2, 128, 128], P('gy', 'gx'), may hold values from 0.05 to 1
Outputs:
- object_grad: float32 [4, 2, 2048, 4096], P(None, None, 'gy', 'gx')
- probe_grad: float32 [2, 128, 128], replicated
Inputs may be any that keep to these rules, and one draw needn't show every extreme that they name: `positions`: slot k of tile (ty, tx) has its corner at row ty * 64 + a and column tx * 256 + b with a between -64 and 0 and b between -64 and 192, moved inward where needed so that the whole patch lies inside the region. `counts`: slots at or above a tile's count are not used.
All inputs are finite; a program needn't handle non-finite values.
Results may differ from a plain program's by a relative error of at most 0.0003.
Values sent between devices are 32-bit elements; how exact they have to be, the bound alone decides.
No kernel may reach another device: no remote copies, remote signals or barrier semaphores. Data moves between devices by JAX's collectives and lax.ppermute only.
A program may use at most 64 MiB of HBM per device.

v0:
```python
import math

import jax
import jax.numpy as jnp
from jax import lax
from jax.sharding import PartitionSpec as P

distance = 0.5
highest = lax.Precision.HIGHEST


def extended_2(cells, sides, width):
    for axis, dim in sides:
        count = lax.axis_size(axis)
        ends = count - 1
        head = lax.slice_in_dim(cells, 0, width, axis=dim)
        tail = lax.slice_in_dim(cells, cells.shape[dim] - width, cells.shape[dim], axis=dim)
        cells = jnp.concatenate(
            [
                lax.ppermute(tail, axis, [(i, (i + 1) % count) for i in range(ends)]),
                cells,
                lax.ppermute(head, axis, [((i + 1) % count, i) for i in range(ends)]),
            ],
            axis=dim,
        )
    return cells


def fourier_tables(patch_size):
    indices = jnp.arange(patch_size)
    angles = (
        2.0
        * math.pi
        / patch_size
        * (indices[:, None] * indices[None, :] % patch_size).astype(jnp.float32)
    )
    norming = 1.0 / math.sqrt(patch_size)
    return (jnp.cos(angles) * norming, -jnp.sin(angles) * norming)


def kernel_tables(patch_size):
    indices = jnp.arange(patch_size)
    frequency = (indices + patch_size // 2) % patch_size - patch_size // 2
    phases = -math.pi * distance / patch_size * (frequency * frequency).astype(jnp.float32)
    summed_phase = phases[:, None] + phases[None, :]
    return (jnp.cos(summed_phase), jnp.sin(summed_phase))


def apply_right(real_part, imag_part, cos_table, sin_table):
    patch_size = cos_table.shape[0]
    wide_table = jnp.concatenate([cos_table, sin_table], axis=1)
    products = jnp.einsum(
        "a...c,ck->a...k", jnp.stack([real_part, imag_part]), wide_table, precision=highest
    )
    new_real = products[0, ..., :patch_size] - products[1, ..., patch_size:]
    new_imag = products[0, ..., patch_size:] + products[1, ..., :patch_size]
    return (new_real, new_imag)


def apply_left(real_part, imag_part, cos_table, sin_table):
    patch_size = cos_table.shape[0]
    tall_table = jnp.concatenate([cos_table, sin_table], axis=0)
    products = jnp.einsum(
        "ur,a...rk->a...uk", tall_table, jnp.stack([real_part, imag_part]), precision=highest
    )
    new_real = products[0, ..., :patch_size, :] - products[1, ..., patch_size:, :]
    new_imag = products[0, ..., patch_size:, :] + products[1, ..., :patch_size, :]
    return (new_real, new_imag)


def transform(pair, tables):
    half_real, half_imag = apply_right(pair[0], pair[1], tables[0], tables[1])
    return apply_left(half_real, half_imag, tables[0], tables[1])


def complex_product(first_pair, second_pair):
    return (
        first_pair[0] * second_pair[0] - first_pair[1] * second_pair[1],
        first_pair[0] * second_pair[1] + first_pair[1] * second_pair[0],
    )


def conj_product(first_pair, second_pair):
    return (
        first_pair[0] * second_pair[0] + first_pair[1] * second_pair[1],
        first_pair[0] * second_pair[1] - first_pair[1] * second_pair[0],
    )


def fold_axis(stacked, axis_dim, length, half_patch):
    middle = lax.slice_in_dim(stacked, 2 * half_patch, 2 * half_patch + length, axis=axis_dim)
    low_rim = lax.slice_in_dim(stacked, 0, half_patch, axis=axis_dim)
    high_rim = lax.slice_in_dim(
        stacked, length + 3 * half_patch, length + 4 * half_patch, axis=axis_dim
    )
    widths_low = [(0, 0)] * stacked.ndim
    widths_low[axis_dim] = (0, length - half_patch)
    widths_high = [(0, 0)] * stacked.ndim
    widths_high[axis_dim] = (length - half_patch, 0)
    return middle + jnp.pad(low_rim, widths_low) + jnp.pad(high_rim, widths_high)


def body(object_slices, probe, positions, counts, measured):
    slices = object_slices.shape[0]
    tile_rows = object_slices.shape[2]
    tile_cols = object_slices.shape[3]
    patch_size = probe.shape[1]
    half_patch = patch_size // 2
    number_of_slots = positions.shape[2]
    zero_index = jnp.zeros((), jnp.int32)
    extended = extended_2(object_slices, (("gx", 3), ("gy", 2)), half_patch)
    row_start = lax.axis_index("gy") * tile_rows - half_patch
    col_start = lax.axis_index("gx") * tile_cols - half_patch
    local_rows = positions[0, 0, :, 0] - row_start
    local_cols = positions[0, 0, :, 1] - col_start

    def extract(first_index, second_index):
        return lax.dynamic_slice(
            extended,
            (zero_index, zero_index, first_index, second_index),
            (slices, 2, patch_size, patch_size),
        )

    windows = jax.vmap(extract)(local_rows, local_cols)
    forward_tables = fourier_tables(patch_size)
    inverse_tables = (forward_tables[0], -forward_tables[1])
    kernel_pair = kernel_tables(patch_size)
    probe_pair = (probe[0], probe[1])
    layers = [(windows[:, s, 0], windows[:, s, 1]) for s in range(slices)]
    current_wave = complex_product(probe_pair, layers[0])
    arriving = []
    for s in range(1, slices):
        spectrum = transform(current_wave, forward_tables)
        propagated = transform(complex_product(kernel_pair, spectrum), inverse_tables)
        arriving.append(propagated)
        current_wave = complex_product(propagated, layers[s])
    far_field = transform(current_wave, forward_tables)
    active_slot_mask = (jnp.arange(number_of_slots) < counts[0, 0]).astype(jnp.float32)[
        :, None, None
    ]
    residual = active_slot_mask * (
        far_field[0] * far_field[0] + far_field[1] * far_field[1] - measured[0, 0]
    )
    backward = transform((residual * far_field[0], residual * far_field[1]), inverse_tables)
    pieces = [None] * slices
    for s in range(slices - 1, 0, -1):
        pieces[s] = conj_product(arriving[s - 1], backward)
        spectrum = transform(conj_product(layers[s], backward), forward_tables)
        backward = transform(conj_product(kernel_pair, spectrum), inverse_tables)
    pieces[0] = conj_product(probe_pair, backward)
    probe_term = conj_product(layers[0], backward)
    updates = jnp.stack([jnp.stack(piece, axis=1) for piece in pieces], axis=1)

    def add_patch(slot, accumulated):
        start = (zero_index, zero_index, local_rows[slot], local_cols[slot])
        current = lax.dynamic_slice(accumulated, start, (slices, 2, patch_size, patch_size))
        return lax.dynamic_update_slice(accumulated, current + updates[slot], start)

    accumulated = lax.fori_loop(
        0, number_of_slots, add_patch, jnp.zeros(extended.shape, jnp.float32)
    )
    arrived = extended_2(accumulated, (("gx", 3), ("gy", 2)), half_patch)
    object_grad = fold_axis(fold_axis(arrived, 2, tile_rows, half_patch), 3, tile_cols, half_patch)
    probe_local = jnp.stack([jnp.sum(probe_term[0], axis=0), jnp.sum(probe_term[1], axis=0)])
    probe_intensity_sum, patches = lax.psum(
        (probe_local, counts[0, 0].astype(jnp.float32)), ("gx", "gy")
    )
    return (object_grad, probe_intensity_sum / patches)


def solution(mesh):
    placed = (
        P(None, None, "gy", "gx"),
        P(),
        P("gy", "gx", None, None),
        P("gy", "gx"),
        P("gy", "gx", None, None, None),
    )
    return jax.shard_map(
        body,
        mesh=mesh,
        in_specs=placed,
        out_specs=(P(None, None, "gy", "gx"), P()),
        check_vma=False,
    )
```

profile of v0, /device:TPU:1, one launch (start us, length us, event | category | flops | bytes accessed | tf_op | source)
XLA Modules:
  0.0 649.6 jit_solution(1458465852617274175)
XLA Ops:
  7.2 1.2 fusion.199
  8.5 4.4 collective-permute-start
  12.8 1.3 collective-permute-start.1
  14.4 1.0 subtract_reduce_fusion
  16.3 1.0 copy.70
  17.6 10.3 %collective-permute-done.1 = f32[4,2,64,64]{3,2,1,0:T(8,128)S(1)} collective-permute-done((f32[4,2,64,64]{3,2,1,0:T(8,128)S(1)}, f32[4,2,64,64]{3,2,1,0:T(8,128)S(1)}, u32[]{:S(2)}, u32[]{:S(2)}) %collective-permute-start.1) | collective-permute-done | bytes 131104 | tf_op jit(solution)/shard_map/ppermute | solution.py:22
  27.8 1.4 pad_maximum_fusion.3
  29.2 2.5 collective-permute-start.3
  31.7 3.1 collective-permute-start.2
  35.2 7.3 %collective-permute-done.3 = f32[4,2,64,384]{3,2,1,0:T(8,128)S(1)} collective-permute-done((f32[4,2,64,384]{3,2,1,0:T(8,128)S(1)}, f32[4,2,64,384]{3,2,1,0:T(8,128)S(1)}, u32[]{:S(2)}, u32[]{:S(2)}) %collective-permute-start.3) | collective-permute-done | bytes 786464 | tf_op jit(solution)/shard_map/ppermute | solution.py:22
  42.5 1.2 collective-permute-done.2
  43.7 1.8 pad_maximum_fusion.1
  45.5 7.0 %while.15 = (s32[]{:T(128)}, f32[4,2,192,384]{3,2,1,0:T(8,128)}, s32[2,4]{1,0:T(2,128)S(1)}, f32[2,4,2,128,128]{4,3,0,2,1:T(8,128)S(1)}, s32[]{:T(128)}) while((s32[]{:T(128)}, f32[4,2,192,384]{3,2,1,0:T(8,128)}, s32[2,4]{1,0:T(2,128)S(1)}, f32[2,4,2,128,128]{4,3,0,2,1:T(8,128)S(1)}, s32[]{:T(128)}) %tuple.100), condition=%wide.while_cond, body=%wide.while_body.sunk | while | flops 2 | bytes 1048709 | solution.py:118
  45.5 0.7 fusion.201
  46.2 2.7 bitcast_dynamic-update-slice_fusion.2
  49.0 0.7 fusion.201
  49.6 2.7 bitcast_dynamic-update-slice_fusion.2
  53.2 0.6 convolution_bitcast_fusion.13
  53.9 0.6 fusion.10
  54.5 0.6 convolution_bitcast_fusion.12
  55.8 0.6 convolution_bitcast_fusion.11
  56.5 0.6 fusion.24
  57.2 0.6 convolution_bitcast_fusion.10
  58.5 0.6 convolution_bitcast_fusion.9
  59.1 0.6 fusion.38
  59.8 0.6 convolution_bitcast_fusion.8
  61.1 0.6 convolution_bitcast_fusion.7
  61.8 0.6 fusion.52
  62.5 0.6 convolution_bitcast_fusion.6
  63.8 0.6 convolution_bitcast_fusion.5
  64.5 0.6 fusion.66
  65.1 0.8 convolution_bitcast_fusion.4
  66.7 0.6 convolution_bitcast_fusion.3
  67.3 0.6 fusion.80
  68.0 0.6 convolution_bitcast_fusion.2
  69.3 0.6 convolution_bitcast_fusion.1
  70.0 0.6 fusion.94
  70.6 0.6 convolution_bitcast_fusion
  71.5 1.1 pad_maximum_fusion.2
  72.7 26.2 %while.14 = (s32[]{:T(128)}, f32[4,2,192,384]{3,2,1,0:T(8,128)S(1)}, s32[2]{0:T(128)S(1)}, s32[2]{0:T(128)S(1)}, f32[2,4,2,128,128]{4,3,0,2,1:T(8,128)}, /*index=5*/s32[]{:T(128)}, s32[]{:T(128)}, s32[]{:T(128)}, s32[]{:T(128)}) while((s32[]{:T(128)}, f32[4,2,192,384]{3,2,1,0:T(8,128)S(1)}, s32[2]{0:T(128)S(1)}, s32[2]{0:T(128)S(1)}, ...), condition=%wide.region_1.2_spmd, body=%wide.region_0.1_spmd.sunk | while | flops 131080 | bytes 2621649 | solution.py:159
  75.3 0.6 dynamic_slice.37
  77.8 1.3 bitcast_add_fusion.2
  79.1 6.8 %dynamic_update_slice.8 = f32[4,2,192,384]{3,2,1,0:T(8,128)S(1)} dynamic-update-slice(f32[4,2,192,384]{3,2,1,0:T(8,128)S(1)} %get-tuple-element.313, f32[4,2,128,128]{3,2,1,0:T(8,128)S(1)} %bitcast_add_fusion.2, s32[]{:T(128)} %constant.80.clone.1..sunk, s32[]{:T(128)} %constant.80.clone.1..sunk, s32[]{:T(128)S(6)} %select_n.152, s32[]{:T(128)S(6)} %select_n.153) | dynamic-update-slice | bytes 1048580 | tf_op jit(solution)/shard_map/while/body/eval_jaxpr/dynamic_update_slice | solution.py:157
  91.0 1.3 bitcast_add_fusion.2
  92.3 6.6 %dynamic_update_slice.8 = f32[4,2,192,384]{3,2,1,0:T(8,128)S(1)} dynamic-update-slice(f32[4,2,192,384]{3,2,1,0:T(8,128)S(1)} %get-tuple-element.313, f32[4,2,128,128]{3,2,1,0:T(8,128)S(1)} %bitcast_add_fusion.2, s32[]{:T(128)} %constant.80.clone.1..sunk, s32[]{:T(128)} %constant.80.clone.1..sunk, s32[]{:T(128)S(6)} %select_n.152, s32[]{:T(128)S(6)} %select_n.153) | dynamic-update-slice | bytes 1048580 | tf_op jit(solution)/shard_map/while/body/eval_jaxpr/dynamic_update_slice | solution.py:157
  98.9 2.3 copy.87
  101.2 2.1 fusion.198
  103.3 2.9 collective-permute-start.4
  106.2 1.3 collective-permute-start.5
  107.5 4.0 collective-permute-done.4
  111.5 1.3 copy.89
  112.8 11.8 %collective-permute-done.5 = f32[4,2,192,64]{2,3,1,0:T(8,128)} collective-permute-done((f32[4,2,192,64]{2,3,1,0:T(8,128)}, f32[4,2,192,64]{2,3,1,0:T(8,128)}, u32[]{:S(2)}, u32[]{:S(2)}) %collective-permute-start.5) | collective-permute-done | bytes 393248 | tf_op jit(solution)/shard_map/ppermute | solution.py:22
  124.6 2.2 copy.90
  126.8 2.2 pad_maximum_fusion
  129.0 1.6 copy-done
  130.7 1.2 fusion.197
  131.9 12.2 %collective-permute-start.6 = (f32[4,2,64,512]{3,2,1,0:T(8,128)}, f32[4,2,64,512]{3,2,1,0:T(8,128)S(1)}, u32[]{:S(2)}, u32[]{:S(2)}) collective-permute-start(f32[4,2,64,512]{3,2,1,0:T(8,128)} %get-tuple-element.159), channel_id=1, source_target_pairs={{0,1},{1,2},{2,3},{3,4},{4,5},{5,6},{6,7},{7,8},{8,9},{9,10},{10,1... | collective-permute-start | bytes 3145736 | tf_op jit(solution)/shard_map/ppermute | solution.py:20
  144.1 1.9 collective-permute-start.7
  146.0 0.7 pad_maximum_fusion.8
  146.7 152.2 %psum.15 = f32[]{:T(128)} all-reduce(f32[]{:T(128)S(6)} %convert_element_type.91), channel_id=1, replica_groups=mesh['gx'=16,'gy'=32] {'gx','gy'}, use_global_device_ids=true, to_apply=%region_5.6 | all-reduce | flops 1 | bytes 8 | tf_op jit(solution)/shard_map/psum | solution.py:165
  298.9 338.9 %all-reduce.3.cloned.1.call-done = f32[2,128,128]{2,1,0:T(8,128)} async-done(((f32[2,128,128]{2,1,0:T(8,128)}), f32[2,128,128]{2,1,0:T(8,128)}) %all-reduce.3.cloned.1.call-update) | async-done | bytes 131088 | tf_op jit(solution)/shard_map/psum | solution.py:165
  637.8 2.2 broadcast_divide_fusion
  640.1 1.6 fusion
  641.8 0.9 fusion.2
  (79 shorter events, 8.8 us)
Async XLA Ops:
  7.2 36.6 %copy-start.1 = (f32[4,2,64,256]{3,2,1,0:T(8,128)S(1)}, f32[4,2,64,256]{3,2,1,0:T(8,128)}, u32[]{:S(2)}) copy-start(f32[4,2,64,256]{3,2,1,0:T(8,128)} %param.7) | copy-start | bytes 1572868
  7.2 28.0 %copy-start.2 = (f32[2,128,128]{2,1,0:T(8,128)S(1)}, f32[2,128,128]{2,1,0:T(8,128)}, u32[]{:S(2)}) copy-start(f32[2,128,128]{2,1,0:T(8,128)} %param.8) | copy-start | bytes 393220
  7.2 630.6 %all-reduce.3.cloned.1.call-start = ((), (), s32[]{:S(2)}) async-start(), calls=%async_computation | async-start | bytes 262144 | tf_op jit(solution)/shard_map/psum | solution.py:165
  8.5 9.1 %collective-permute-start = (f32[4,2,64,64]{3,2,1,0:T(8,128)S(1)}, f32[4,2,64,64]{3,2,1,0:T(8,128)S(1)}, u32[]{:S(2)}, u32[]{:S(2)}) collective-permute-start(f32[4,2,64,64]{3,2,1,0:T(8,128)S(1)} %get-tuple-element.213), channel_id=1, source_target_pairs={{0,32},{32,64},{64,96},{96,128},{128,160},{160,192},{192,224},{224... | collective-permute-start | bytes 393224 | tf_op jit(solution)/shard_map/ppermute | solution.py:20
  12.8 15.0 %collective-permute-start.1 = (f32[4,2,64,64]{3,2,1,0:T(8,128)S(1)}, f32[4,2,64,64]{3,2,1,0:T(8,128)S(1)}, u32[]{:S(2)}, u32[]{:S(2)}) collective-permute-start(f32[4,2,64,64]{3,2,1,0:T(8,128)S(1)} %get-tuple-element.214), channel_id=1, source_target_pairs={{32,0},{64,32},{96,64},{128,96},{160,128},{192,160},{224,192},{256... | collective-permute-start | bytes 393224 | tf_op jit(solution)/shard_map/ppermute | solution.py:22
  29.2 13.3 %collective-permute-start.3 = (f32[4,2,64,384]{3,2,1,0:T(8,128)S(1)}, f32[4,2,64,384]{3,2,1,0:T(8,128)S(1)}, u32[]{:S(2)}, u32[]{:S(2)}) collective-permute-start(f32[4,2,64,384]{3,2,1,0:T(8,128)S(1)} %pad_maximum_fusion.3), channel_id=1, source_target_pairs={{1,0},{2,1},{3,2},{4,3},{5,4},{6,5},{7,6},{8,7},{9,8},{10,9},{11,1... | collective-permute-start | bytes 2359304 | tf_op jit(solution)/shard_map/ppermute | solution.py:22
  31.7 12.0 %collective-permute-start.2 = (f32[4,2,64,384]{3,2,1,0:T(8,128)S(1)}, f32[4,2,64,384]{3,2,1,0:T(8,128)S(1)}, u32[]{:S(2)}, u32[]{:S(2)}) collective-permute-start(f32[4,2,64,384]{3,2,1,0:T(8,128)S(1)} %pad_maximum_fusion.3), channel_id=1, source_target_pairs={{0,1},{1,2},{2,3},{3,4},{4,5},{5,6},{6,7},{7,8},{8,9},{9,10},{10,1... | collective-permute-start | bytes 2359304 | tf_op jit(solution)/shard_map/ppermute | solution.py:20
  103.3 8.2 %collective-permute-start.4 = (f32[4,2,192,64]{2,3,1,0:T(8,128)S(1)}, f32[4,2,192,64]{2,3,1,0:T(8,128)}, u32[]{:S(2)}, u32[]{:S(2)}) collective-permute-start(f32[4,2,192,64]{2,3,1,0:T(8,128)S(1)} %get-tuple-element.161), channel_id=1, source_target_pairs={{0,32},{32,64},{64,96},{96,128},{128,160},{160,192},{192,224},{224... | collective-permute-start | bytes 1179656 | tf_op jit(solution)/shard_map/ppermute | solution.py:20
  106.2 18.4 %collective-permute-start.5 = (f32[4,2,192,64]{2,3,1,0:T(8,128)}, f32[4,2,192,64]{2,3,1,0:T(8,128)}, u32[]{:S(2)}, u32[]{:S(2)}) collective-permute-start(f32[4,2,192,64]{2,3,1,0:T(8,128)} %get-tuple-element.162), channel_id=1, source_target_pairs={{32,0},{64,32},{96,64},{128,96},{160,128},{192,160},{224,192},{256... | collective-permute-start | bytes 1179656 | tf_op jit(solution)/shard_map/ppermute | solution.py:22
  129.0 1.6 copy-start
  131.9 508.2 %collective-permute-start.6 = (f32[4,2,64,512]{3,2,1,0:T(8,128)}, f32[4,2,64,512]{3,2,1,0:T(8,128)S(1)}, u32[]{:S(2)}, u32[]{:S(2)}) collective-permute-start(f32[4,2,64,512]{3,2,1,0:T(8,128)} %get-tuple-element.159), channel_id=1, source_target_pairs={{0,1},{1,2},{2,3},{3,4},{4,5},{5,6},{6,7},{7,8},{8,9},{9,10},{10,1... | collective-permute-start | bytes 3145736 | tf_op jit(solution)/shard_map/ppermute | solution.py:20
  144.1 496.0 %collective-permute-start.7 = (f32[4,2,64,512]{3,2,1,0:T(8,128)S(1)}, f32[4,2,64,512]{3,2,1,0:T(8,128)S(1)}, u32[]{:S(2)}, u32[]{:S(2)}) collective-permute-start(f32[4,2,64,512]{3,2,1,0:T(8,128)S(1)} %get-tuple-element.160), channel_id=1, source_target_pairs={{1,0},{2,1},{3,2},{4,3},{5,4},{6,5},{7,6},{8,7},{9,8},{10,9},{11,1... | collective-permute-start | bytes 3145736 | tf_op jit(solution)/shard_map/ppermute | solution.py:22
  640.0 1.7 copy-start.3
Sparse Core Ops, SparseCore 0:
  146.8 490.9 all-reduce.2
where the time goes:
time: 651 us; the launch traced here: 650 us
  waiting for transfers between devices  373 us (57%)
  blocking collectives  152 us (23%)
  local copies, waits for them, and re-layouts  36.1 us (6%)
  starting transfers between devices  29.6 us (5%)
  other arithmetic  17.9 us (3%)
  matrix products  16.9 us (3%)
  between operations  15.4 us (2%)
  loops' own time  8.03 us (1%)
    psum x1, waiting for transfers between devices, body(): lax.psum((probe_local, counts[0, 0].astype(jnp.float32)), ('gx', 'gy'))  339 us
    psum x1, blocking collectives, body(): lax.psum((probe_local, counts[0, 0].astype(jnp.float32)), ('gx', 'gy'))  152 us
    ppermute x4, waiting for transfers between devices, extended_2(): lax.ppermute(head, axis, [((i + 1) % count, i) for i in range(ends)])  29.4 us
    ppermute x4, starting transfers between devices, extended_2(): lax.ppermute(tail, axis, [(i, (i + 1) % count) for i in range(ends)])  22.6 us
    dynamic_update_slice x2, local copies, waits for them, and re-layouts, add_patch(): return lax.dynamic_update_slice(accumulated, current + updates[slot], start)  13.5 us
  transfers between devices with their start and end apart: 9, of which 6 were waited for; matrix products, arithmetic and copies ran while one was open for 1% of the time, Pallas kernels for 0%

commit v1 on v0

v1 whole, which is shorter than its diff:
```python
import math

import jax
import jax.numpy as jnp
import ml_dtypes
import numpy as np
from jax import lax
from jax.experimental import pallas as pl
from jax.experimental.pallas import tpu as pltpu
from jax.sharding import PartitionSpec as P

distance = 0.5
SIDE = 128
HALF = 64
SLICES = 4
SLOTS = 2
RUN = 8
Z_HI, Z_LO, N_X = 4, 4, 4


def split_table(matrix):
    real, imag = matrix.real, matrix.imag
    right = np.block([[real, imag], [-imag, real]]).astype(np.float32)
    parts = []
    for table in (right, right.T):
        high = table.astype(ml_dtypes.bfloat16)
        low = (table - high.astype(np.float32)).astype(ml_dtypes.bfloat16)
        parts.append(np.stack([high, low]))
    return np.stack(parts)


def tables():
    indices = np.arange(SIDE)
    fourier = np.exp(-2j * math.pi / SIDE * (np.outer(indices, indices) % SIDE)) / math.sqrt(SIDE)
    frequency = (indices + SIDE // 2) % SIDE - SIDE // 2
    phase = np.exp(-1j * math.pi * distance / SIDE * frequency * frequency)
    propagator = np.conj(fourier) @ (phase[:, None] * fourier)
    return np.stack([split_table(propagator), split_table(fourier)])


def split_value(value):
    high = value.astype(jnp.bfloat16)
    return high, (value - high.astype(jnp.float32)).astype(jnp.bfloat16)


def two_sided(fields, table_ref, which, conjugate):
    first, second = (1, 0) if conjugate else (0, 1)
    slots = len(fields)
    stacked = jnp.concatenate([jnp.concatenate(pair, axis=1) for pair in fields], axis=0)
    high, low = split_value(stacked)
    w_high, w_low = table_ref[which, first, 0], table_ref[which, first, 1]
    half = jnp.dot(
        jnp.concatenate([high, low, high], axis=1),
        jnp.concatenate([w_high, w_high, w_low], axis=0),
        preferred_element_type=jnp.float32,
    )
    rows = []
    for part in range(2):
        rows.append(
            jnp.concatenate(
                [half[k * SIDE : (k + 1) * SIDE, part * SIDE : (part + 1) * SIDE] for k in range(slots)],
                axis=1,
            )
        )
    high, low = split_value(jnp.concatenate(rows, axis=0))
    w_high, w_low = table_ref[which, second, 0], table_ref[which, second, 1]
    full = jnp.dot(
        jnp.concatenate([w_high, w_high, w_low], axis=1),
        jnp.concatenate([high, low, high], axis=0),
        preferred_element_type=jnp.float32,
    )
    return [
        (full[:SIDE, k * SIDE : (k + 1) * SIDE], full[SIDE:, k * SIDE : (k + 1) * SIDE])
        for k in range(slots)
    ]


def times(a, b):
    return (a[0] * b[0] - a[1] * b[1], a[0] * b[1] + a[1] * b[0])


def conj_times(a, b):
    return (a[0] * b[0] + a[1] * b[1], a[0] * b[1] - a[1] * b[0])


def patch_kernel(
    corner_ref,
    count_ref,
    own_ref,
    edge_up_ref,
    edge_down_ref,
    mid_up_ref,
    mid_down_ref,
    rim_left_ref,
    rim_right_ref,
    probe_ref,
    measured_ref,
    table_ref,
    own_out,
    edge_up_out,
    edge_down_out,
    mid_up_out,
    mid_down_out,
    rim_left_out,
    rim_right_out,
    payload_out,
    extended,
    windows,
    waves,
    total,
):
    low_lanes = lax.broadcasted_iota(jnp.int32, (HALF, SIDE), 1) < HALF
    for s in range(SLICES):
        for c in range(2):
            extended[s, c, 1, HALF : 2 * HALF, :] = own_ref[s, c, :, :SIDE]
            extended[s, c, 2, HALF : 2 * HALF, :] = own_ref[s, c, :, SIDE:]
            for b, edge_ref, mid_ref in ((0, edge_up_ref, mid_up_ref), (2, edge_down_ref, mid_down_ref)):
                edge, mid = edge_ref[s, c], mid_ref[s, c]
                extended[s, c, 1, b * HALF : (b + 1) * HALF, :] = jnp.where(low_lanes, edge, mid)
                extended[s, c, 2, b * HALF : (b + 1) * HALF, :] = jnp.where(low_lanes, mid, edge)
        for b in range(3):
            left, right = rim_left_ref[s, b], rim_right_ref[s, b]
            extended[s, 0, 0, b * HALF : (b + 1) * HALF, :] = pltpu.roll(left, HALF, 1)
            extended[s, 1, 0, b * HALF : (b + 1) * HALF, :] = left
            extended[s, 0, 3, b * HALF : (b + 1) * HALF, :] = right
            extended[s, 1, 3, b * HALF : (b + 1) * HALF, :] = pltpu.roll(right, HALF, 1)

    lanes = lax.broadcasted_iota(jnp.int32, (SIDE, SIDE), 1)
    places = []
    for k in range(SLOTS):
        row, col = corner_ref[k, 0], corner_ref[k, 1] + HALF
        places.append((row, col // SIDE, col % SIDE))
    for k in range(SLOTS):
        row, block, shift = places[k]
        back = (SIDE - shift) % SIDE
        inside = lanes < SIDE - shift
        for s in range(SLICES):
            for c in range(2):
                near = extended[s, c, block, pl.ds(row, SIDE), :]
                far = extended[s, c, block + 1, pl.ds(row, SIDE), :]
                windows[k, s, c] = jnp.where(inside, pltpu.roll(near, back, 1), pltpu.roll(far, back, 1))

    probe = (probe_ref[0], probe_ref[1])

    def layer(k, s):
        return (windows[k, s, 0], windows[k, s, 1])

    slots = range(SLOTS)
    fields = [times(probe, layer(k, 0)) for k in slots]
    for s in range(1, SLICES):
        arrived = two_sided(fields, table_ref, 0, False)
        for k in slots:
            waves[k, s - 1, 0] = arrived[k][0]
            waves[k, s - 1, 1] = arrived[k][1]
        fields = [times(arrived[k], layer(k, s)) for k in slots]
    far_fields = two_sided(fields, table_ref, 1, False)
    scaled = []
    for k in slots:
        real, imag = far_fields[k]
        residual = jnp.where(k < count_ref[0], real * real + imag * imag - measured_ref[k], 0.0)
        scaled.append((residual * real, residual * imag))
    backward = two_sided(scaled, table_ref, 1, True)

    total[...] = jnp.zeros_like(total)

    def add(k, s, pair):
        row, block, shift = places[k]
        inside = lanes >= shift
        for c in range(2):
            moved = pltpu.roll(pair[c], shift, 1)
            total[s, c, block, pl.ds(row, SIDE), :] += jnp.where(inside, moved, 0.0)
            total[s, c, block + 1, pl.ds(row, SIDE), :] += jnp.where(inside, 0.0, moved)

    for s in range(SLICES - 1, 0, -1):
        for k in slots:
            add(k, s, conj_times((waves[k, s - 1, 0], waves[k, s - 1, 1]), backward[k]))
        backward = two_sided([conj_times(layer(k, s), backward[k]) for k in slots], table_ref, 0, True)
    for k in slots:
        add(k, 0, conj_times(probe, backward[k]))
    terms = [conj_times(layer(k, 0), backward[k]) for k in slots]
    for c in range(2):
        summed = (terms[0][c] + terms[1][c]).reshape(16, 8, SIDE)
        payload_out[c * 16 : (c + 1) * 16, 0:8, :] = summed
    payload_out[:, 8:16, :] = jnp.full((32, 8, SIDE), count_ref[0].astype(jnp.float32), jnp.float32)

    for s in range(SLICES):
        for c in range(2):
            own_out[s, c, :, :SIDE] = total[s, c, 1, HALF : 2 * HALF, :]
            own_out[s, c, :, SIDE:] = total[s, c, 2, HALF : 2 * HALF, :]
            for b, edge_out, mid_out in ((0, edge_up_out, mid_up_out), (2, edge_down_out, mid_down_out)):
                first = total[s, c, 1, b * HALF : (b + 1) * HALF, :]
                second = total[s, c, 2, b * HALF : (b + 1) * HALF, :]
                edge_out[s, c] = jnp.where(low_lanes, first, second)
                mid_out[s, c] = jnp.where(low_lanes, second, first)
        for b in range(3):
            rows = slice(b * HALF, (b + 1) * HALF)
            rim_left_out[s, b] = jnp.where(
                low_lanes, pltpu.roll(total[s, 0, 0, rows, :], HALF, 1), total[s, 1, 0, rows, :]
            )
            rim_right_out[s, b] = jnp.where(
                low_lanes, total[s, 0, 3, rows, :], pltpu.roll(total[s, 1, 3, rows, :], HALF, 1)
            )


def gradients(corners, count, own, edge_up, edge_down, mid_up, mid_down, rim_left, rim_right, probe, measured, table):
    f32 = jnp.float32
    band = jax.ShapeDtypeStruct((SLICES, 2, HALF, SIDE), f32)
    rim = jax.ShapeDtypeStruct((SLICES, 3, HALF, SIDE), f32)
    vmem = pl.BlockSpec(memory_space=pltpu.VMEM)
    smem = pl.BlockSpec(memory_space=pltpu.SMEM)
    return pl.pallas_call(
        patch_kernel,
        out_shape=[
            jax.ShapeDtypeStruct((SLICES, 2, HALF, 2 * SIDE), f32),
            band,
            band,
            band,
            band,
            rim,
            rim,
            jax.ShapeDtypeStruct((32, 16, SIDE), f32),
        ],
        in_specs=[smem, smem] + [vmem] * 10,
        out_specs=[vmem] * 8,
        scratch_shapes=[
            pltpu.VMEM((SLICES, 2, 4, 3 * HALF, SIDE), f32),
            pltpu.VMEM((SLOTS, SLICES, 2, SIDE, SIDE), f32),
            pltpu.VMEM((SLOTS, SLICES - 1, 2, SIDE, SIDE), f32),
            pltpu.VMEM((SLICES, 2, 4, 3 * HALF, SIDE), f32),
        ],
        compiler_params=pltpu.CompilerParams(vmem_limit_bytes=40 * 1024 * 1024),
    )(corners, count, own, edge_up, edge_down, mid_up, mid_down, rim_left, rim_right, probe, measured, table)


def pairs(count, step):
    return [(i, step(i)) for i in range(count) if step(i) is not None and 0 <= step(i) < count]


def hop_down(mid, count):
    far = lax.ppermute(mid, "gy", pairs(count, lambda i: i + RUN if i % RUN == RUN - 1 else None))
    here = lax.axis_index("gy") % RUN == RUN - 1
    step = lambda i: i + 1 if i % RUN != RUN - 1 else (i - RUN + 1 if i >= RUN else None)
    return lax.ppermute(jnp.where(here, far, mid), "gy", pairs(count, step))


def hop_up(mid, count):
    far = lax.ppermute(mid, "gy", pairs(count, lambda i: i - RUN if i % RUN == 0 else None))
    here = lax.axis_index("gy") % RUN == 0
    step = lambda i: i - 1 if i % RUN != 0 else (i + RUN - 1 if i < count - RUN else None)
    return lax.ppermute(jnp.where(here, far, mid), "gy", pairs(count, step))


def near_groups():
    return [
        [(x * Z_LO + low) * Z_HI * RUN + high * RUN + m for x in range(N_X) for m in range(RUN)]
        for low in range(Z_LO)
        for high in range(Z_HI)
    ]


def far_groups():
    return [
        [(x * Z_LO + low) * Z_HI * RUN + high * RUN + m for high in range(Z_HI) for low in range(Z_LO)]
        for x in range(N_X)
        for m in range(RUN)
    ]


def exchange(pieces, groups):
    return lax.all_to_all(pieces, ("gx", "gy"), 0, 0, tiled=True, axis_index_groups=groups)


def body(object_slices, probe, positions, counts, measured):
    n_gy, n_gx = lax.axis_size("gy"), lax.axis_size("gx")
    down = pairs(n_gy, lambda i: i + 1)
    up = pairs(n_gy, lambda i: i - 1)
    right = pairs(n_gx, lambda i: i + 1)
    left = pairs(n_gx, lambda i: i - 1)
    cols = object_slices.shape[3]

    mid = jnp.concatenate([object_slices[..., SIDE : SIDE + HALF], object_slices[..., HALF:SIDE]], axis=3)
    edge = jnp.concatenate([object_slices[..., :HALF], object_slices[..., cols - HALF :]], axis=3)
    mid_up = hop_down(mid, n_gy)
    mid_down = hop_up(mid, n_gy)
    edge_up = lax.ppermute(edge, "gy", down)
    edge_down = lax.ppermute(edge, "gy", up)
    bands = jnp.stack([edge_up, edge, edge_down], axis=1)
    lefts = jnp.concatenate([bands[:, :, 0, :, :HALF], bands[:, :, 1, :, :HALF]], axis=3)
    rights = jnp.concatenate([bands[:, :, 0, :, HALF:], bands[:, :, 1, :, HALF:]], axis=3)
    rim_left = lax.ppermute(rights, "gx", right)
    rim_right = lax.ppermute(lefts, "gx", left)

    start = jnp.stack([lax.axis_index("gy") * HALF, lax.axis_index("gx") * cols]).astype(jnp.int32)
    corners = positions[0, 0] - start[None, :] + HALF
    own, edge_up, edge_down, mid_up, mid_down, rim_left, rim_right, payload = gradients(
        corners,
        counts[0],
        object_slices,
        edge_up,
        edge_down,
        mid_up,
        mid_down,
        rim_left,
        rim_right,
        probe,
        measured[0, 0],
        jnp.asarray(tables()),
    )

    from_right = lax.ppermute(rim_left, "gx", left)
    from_left = lax.ppermute(rim_right, "gx", right)
    mid_sum = hop_up(mid_up, n_gy) + hop_down(mid_down, n_gy)

    def rim_bands(b):
        return jnp.stack(
            [
                jnp.concatenate([from_left[:, b, :, :HALF], from_right[:, b, :, :HALF]], axis=2),
                jnp.concatenate([from_left[:, b, :, HALF:], from_right[:, b, :, HALF:]], axis=2),
            ],
            axis=1,
        )

    edge_sum = (
        lax.ppermute(edge_up + rim_bands(0), "gy", up)
        + lax.ppermute(edge_down + rim_bands(2), "gy", down)
        + rim_bands(1)
    )

    near, far = near_groups(), far_groups()
    part = jnp.sum(exchange(payload, near), axis=0)
    part = jnp.sum(exchange(jnp.broadcast_to(part, (Z_LO * Z_HI, 16, SIDE)), far), axis=0)
    part = part[:8] / part[8:]
    probe_grad = exchange(jnp.broadcast_to(part, (32, 8, SIDE)), near).reshape(2, SIDE, SIDE)

    object_grad = own + jnp.concatenate(
        [edge_sum[..., :HALF], mid_sum[..., HALF:], mid_sum[..., :HALF], edge_sum[..., HALF:]], axis=3
    )
    return object_grad, probe_grad


def solution(mesh):
    placed = (
        P(None, None, "gy", "gx"),
        P(),
        P("gy", "gx", None, None),
        P("gy", "gx"),
        P("gy", "gx", None, None, None),
    )
    return jax.shard_map(
        body,
        mesh=mesh,
        in_specs=placed,
        out_specs=(P(None, None, "gy", "gx"), P()),
        check_vma=False,
    )
```

time: 651 us -> 155 us (0.24)
  the two profiles are of different devices: /device:TPU:1 before, /device:TPU:481 now
where the time goes in v1:
time: 155 us; the launch traced here: 154 us
  starting transfers between devices  112 us (72%)
  waiting for transfers between devices  25.8 us (17%)
  Pallas kernels  7.5 us (5%)
  local copies, waits for them, and re-layouts  4.42 us (3%)
  other arithmetic  2.7 us (2%)
  between operations  1.75 us (1%)
    all_to_all x3, starting transfers between devices, exchange(): lax.all_to_all(pieces, ('gx', 'gy'), 0, 0, tiled=True, axis_index_groups=...  42.8 us
    ppermute x2, starting transfers between devices, hop_up(): return lax.ppermute(jnp.where(here, far, mid), 'gy', pairs(count, step))  33.2 us
    ppermute x1, waiting for transfers between devices, body(): lax.ppermute(edge_down + rim_bands(2), 'gy', down)  8.64 us
    pallas_call x1, Pallas kernels, gradients(): pl.pallas_call(patch_kernel, out_shape=[jax.ShapeDtypeStruct((SLICES, 2,...  7.5 us
    all_to_all x3, waiting for transfers between devices, exchange(): lax.all_to_all(pieces, ('gx', 'gy'), 0, 0, tiled=True, axis_index_groups=...  6.64 us
    ppermute x1, starting transfers between devices, body(): rim_left = lax.ppermute(rights, 'gx', right)  4.45 us
    ppermute x1, starting transfers between devices, body(): from_left = lax.ppermute(rim_right, 'gx', right)  4.3 us
    ppermute x1, starting transfers between devices, body(): from_right = lax.ppermute(rim_left, 'gx', left)  4.15 us
  transfers between devices with their start and end apart: 19, of which 7 were waited for; matrix products, arithmetic and copies ran while one was open for 3% of the time, Pallas kernels for 0%

profile of v1, /device:TPU:481, one launch (start us, length us, event | category | flops | bytes accessed | tf_op | source)
XLA Modules:
  0.0 153.9 jit_solution(13485951642467588628)
XLA Ops:
  0.6 1.4 fusion.1
  2.0 0.1 copy_bitcast_fusion
  2.2 2.6 %collective-permute-start.1 = (f32[4,2,64,128]{3,2,0,1:T(8,128)S(1)}, f32[4,2,64,128]{3,2,0,1:T(8,128)S(1)}, u32[]{:S(2)}, u32[]{:S(2)}) collective-permute-start(f32[4,2,64,128]{3,2,0,1:T(8,128)S(1)} %get-tuple-element.43), channel_id=1, source_target_pairs={{1,0},{2,1},{3,2},{4,3},{5,4},{6,5},{7,6},{8,7},{9,8},{10,9},{11,1... | collective-permute-start | bytes 786440 | tf_op jit(solution)/shard_map/ppermute | solution.py:286
  4.8 3.1 %collective-permute-start = (f32[4,2,64,128]{3,2,0,1:T(8,128)S(1)}, f32[4,2,64,128]{3,2,0,1:T(8,128)S(1)}, u32[]{:S(2)}, u32[]{:S(2)}) collective-permute-start(f32[4,2,64,128]{3,2,0,1:T(8,128)S(1)} %get-tuple-element.43), channel_id=1, source_target_pairs={{0,1},{1,2},{2,3},{3,4},{4,5},{5,6},{6,7},{7,8},{8,9},{9,10},{10,1... | collective-permute-start | bytes 786440 | tf_op jit(solution)/shard_map/ppermute | solution.py:285
  7.9 0.1 pad_maximum_fusion.4
  8.0 0.7 collective-permute-start.4
  8.7 0.7 collective-permute-start.2
  9.4 0.6 collective-permute-done.1
  10.0 3.1 %collective-permute-done = f32[4,2,64,128]{3,2,0,1:T(8,128)S(1)} collective-permute-done((f32[4,2,64,128]{3,2,0,1:T(8,128)S(1)}, f32[4,2,64,128]{3,2,0,1:T(8,128)S(1)}, u32[]{:S(2)}, u32[]{:S(2)}) %collective-permute-start) | collective-permute-done | bytes 262176 | tf_op jit(solution)/shard_map/ppermute | solution.py:285
  13.1 0.1 pad_maximum_fusion
  13.2 0.3 slice_bitcast_fusion.1
  13.5 0.2 pad_maximum_fusion.1
  13.7 4.5 %collective-permute-start.6 = (f32[4,3,64,128]{3,2,1,0:T(8,128)S(1)}, f32[4,3,64,128]{3,2,1,0:T(8,128)S(1)}, u32[]{:S(2)}, u32[]{:S(2)}) collective-permute-start(f32[4,3,64,128]{3,2,1,0:T(8,128)S(1)} %pad_maximum_fusion.1), channel_id=1, source_target_pairs={{0,32},{32,64},{64,96},{96,128},{128,160},{160,192},{192,224},{224... | collective-permute-start | bytes 1179656 | tf_op jit(solution)/shard_map/ppermute | solution.py:290
  18.1 0.2 pad_maximum_fusion.2
  18.3 0.0 copy-start.1
  18.3 2.1 %collective-permute-start.7 = (f32[4,3,64,128]{3,2,1,0:T(8,128)S(1)}, f32[4,3,64,128]{3,2,1,0:T(8,128)S(1)}, u32[]{:S(2)}, u32[]{:S(2)}) collective-permute-start(f32[4,3,64,128]{3,2,1,0:T(8,128)S(1)} %pad_maximum_fusion.2), channel_id=1, source_target_pairs={{32,0},{64,32},{96,64},{128,96},{160,128},{192,160},{224,192},{256... | collective-permute-start | bytes 1179656 | tf_op jit(solution)/shard_map/ppermute | solution.py:291
  20.4 0.0 collective-permute-done.4
  20.4 0.0 collective-permute-done.2
  20.4 0.1 broadcast_select_fusion.1
  20.6 29.6 %collective-permute-start.5 = (f32[4,2,64,128]{3,2,1,0:T(8,128)S(1)}, f32[4,2,64,128]{3,2,1,0:T(8,128)S(1)}, u32[]{:S(2)}, u32[]{:S(2)}) collective-permute-start(f32[4,2,64,128]{3,2,1,0:T(8,128)S(1)} %get-tuple-element.44), channel_id=1, source_target_pairs={{0,7},{1,0},{2,1},{3,2},{4,3},{5,4},{6,5},{7,6},{8,15},{9,8},{10,9... | collective-permute-start | bytes 786440 | tf_op jit(solution)/shard_map/ppermute | solution.py:250
  50.2 1.9 %collective-permute-start.3 = (f32[4,2,64,128]{3,2,1,0:T(8,128)S(1)}, f32[4,2,64,128]{3,2,1,0:T(8,128)S(1)}, u32[]{:S(2)}, u32[]{:S(2)}) collective-permute-start(f32[4,2,64,128]{3,2,1,0:T(8,128)S(1)} %get-tuple-element.45), channel_id=1, source_target_pairs={{0,1},{1,2},{2,3},{3,4},{4,5},{5,6},{6,7},{8,9},{9,10},{10,11},{11... | collective-permute-start | bytes 786440 | tf_op jit(solution)/shard_map/ppermute | solution.py:243
  52.1 0.1 pad_add_fusion
  52.9 0.0 copy-done.4
  52.9 0.0 copy-start
  52.9 0.0 copy-start.2
  52.9 0.0 copy-start.3
  53.0 0.0 collective-permute-done.5.mid_down_ref
  53.0 2.4 %collective-permute-done.3.mid_up_ref = f32[4,2,64,128]{3,2,1,0:T(8,128)S(1)} collective-permute-done((f32[4,2,64,128]{3,2,1,0:T(8,128)S(1)}, f32[4,2,64,128]{3,2,1,0:T(8,128)S(1)}, u32[]{:S(2)}, u32[]{:S(2)}) %collective-permute-start.3) | collective-permute-done | bytes 262176 | tf_op jit(solution)/shard_map/ppermute | solution.py:243
  55.4 0.0 collective-permute-done.6.rim_left_ref
  55.4 0.0 collective-permute-done.7.rim_right_ref
  55.5 7.5 %shard_map.77 = (f32[4,2,64,256]{3,2,1,0:T(8,128)S(1)}, f32[4,2,64,128]{3,2,1,0:T(8,128)S(1)}, f32[4,2,64,128]{3,2,1,0:T(8,128)S(1)}, f32[4,2,64,128]{3,2,1,0:T(...) custom-call(s32[2,2]{1,0:T(2,128)S(1)} %fusion.corner_ref, ...), custom_call_target="tpu_custom_call" | custom-call | tf_op jit(solution)/shard_map/pallas_call | solution.py:211
  63.0 1.3 collective-permute-start.12
  64.3 8.0 %all-to-all-start = ((f32[32,16,128]{2,1,0:T(8,128)}), f32[32,16,128]{2,1,0:T(8,128)S(1)}, u32[]{:S(2)}, u32[]{:S(2)}) async-start(f32[32,16,128]{2,1,0:T(8,128)} %get-tuple-element.17), calls=%async_computation | async-start | bytes 524288 | tf_op jit(solution)/shard_map/all_to_all | solution.py:270
  72.3 1.4 collective-permute-start.14
  73.7 4.2 %collective-permute-start.9 = (f32[4,3,64,128]{3,2,0,1:T(8,128)S(1)}, f32[4,3,64,128]{3,2,0,1:T(8,128)S(1)}, u32[]{:S(2)}, u32[]{:S(2)}) collective-permute-start(f32[4,3,64,128]{3,2,0,1:T(8,128)S(1)} %copy.27), channel_id=1, source_target_pairs={{32,0},{64,32},{96,64},{128,96},{160,128},{192,160},{224,192},{256... | collective-permute-start | bytes 1179656 | tf_op jit(solution)/shard_map/ppermute | solution.py:310
  77.9 4.3 %collective-permute-start.8 = (f32[4,3,64,128]{3,2,0,1:T(8,128)S(1)}, f32[4,3,64,128]{3,2,0,1:T(8,128)S(1)}, u32[]{:S(2)}, u32[]{:S(2)}) collective-permute-start(f32[4,3,64,128]{3,2,0,1:T(8,128)S(1)} %copy.26), channel_id=1, source_target_pairs={{0,32},{32,64},{64,96},{96,128},{128,160},{160,192},{192,224},{224... | collective-permute-start | bytes 1179656 | tf_op jit(solution)/shard_map/ppermute | solution.py:311
  82.2 0.0 all-to-all-done
  82.2 0.7 broadcast_in_dim.7
  82.9 6.9 %all-to-all-start.1 = ((f32[16,16,128]{2,1,0:T(8,128)}), f32[16,16,128]{2,1,0:T(8,128)S(1)}, u32[]{:S(2)}, u32[]{:S(2)}) async-start(f32[16,16,128]{2,1,0:T(8,128)} %broadcast_in_dim.7), calls=%async_computation.1 | async-start | bytes 262144 | tf_op jit(solution)/shard_map/all_to_all | solution.py:270
  89.8 0.0 collective-permute-done.12
  89.9 3.6 %collective-permute-start.13 = (f32[4,2,64,128]{3,2,1,0:T(8,128)S(1)}, f32[4,2,64,128]{3,2,1,0:T(8,128)S(1)}, u32[]{:S(2)}, u32[]{:S(2)}) collective-permute-start(f32[4,2,64,128]{3,2,1,0:T(8,128)S(1)} %broadcast_select_fusion), channel_id=1, source_target_pairs={{0,7},{1,0},{2,1},{3,2},{4,3},{5,4},{6,5},{7,6},{8,15},{9,8},{10,9... | collective-permute-start | bytes 786440 | tf_op jit(solution)/shard_map/ppermute | solution.py:250
  93.5 0.0 collective-permute-done.14
  93.5 2.1 %collective-permute-start.15 = (f32[4,2,64,128]{3,2,1,0:T(8,128)S(1)}, f32[4,2,64,128]{3,2,1,0:T(8,128)S(1)}, u32[]{:S(2)}, u32[]{:S(2)}) collective-permute-start(f32[4,2,64,128]{3,2,1,0:T(8,128)S(1)} %broadcast_select_fusion.2), channel_id=1, source_target_pairs={{0,1},{1,2},{2,3},{3,4},{4,5},{5,6},{6,7},{8,9},{9,10},{10,11},{11... | collective-permute-start | bytes 786440 | tf_op jit(solution)/shard_map/ppermute | solution.py:243
  95.6 0.0 collective-permute-done.9
  95.6 0.2 slice_bitcast_fusion.10
  95.8 2.7 %collective-permute-done.8 = f32[4,3,64,128]{3,2,0,1:T(8,128)S(1)} collective-permute-done((f32[4,3,64,128]{3,2,0,1:T(8,128)S(1)}, f32[4,3,64,128]{3,2,0,1:T(8,128)S(1)}, u32[]{:S(2)}, u32[]{:S(2)}) %collective-permute-start.8) | collective-permute-done | bytes 393248 | tf_op jit(solution)/shard_map/ppermute | solution.py:311
  98.5 0.2 slice_bitcast_fusion.11
  98.7 0.1 maximum_bitcast_fusion
  98.9 3.6 %collective-permute-start.10 = (f32[4,2,64,128]{3,2,0,1:T(8,128)S(1)}, f32[4,2,64,128]{3,2,0,1:T(8,128)S(1)}, u32[]{:S(2)}, u32[]{:S(2)}) collective-permute-start(f32[4,2,64,128]{3,2,0,1:T(8,128)S(1)} %maximum_add_fusion.1), channel_id=1, source_target_pairs={{1,0},{2,1},{3,2},{4,3},{5,4},{6,5},{7,6},{8,7},{9,8},{10,9},{11,1... | collective-permute-start | bytes 786440 | tf_op jit(solution)/shard_map/ppermute | solution.py:324
  102.5 0.1 maximum_bitcast_fusion.2
  102.7 3.5 %collective-permute-start.11 = (f32[4,2,64,128]{3,2,0,1:T(8,128)S(1)}, f32[4,2,64,128]{3,2,0,1:T(8,128)S(1)}, u32[]{:S(2)}, u32[]{:S(2)}) collective-permute-start(f32[4,2,64,128]{3,2,0,1:T(8,128)S(1)} %maximum_add_fusion.2), channel_id=1, source_target_pairs={{0,1},{1,2},{2,3},{3,4},{4,5},{5,6},{6,7},{7,8},{8,9},{9,10},{10,1... | collective-permute-start | bytes 786440 | tf_op jit(solution)/shard_map/ppermute | solution.py:325
  106.1 0.1 maximum_bitcast_fusion.4
  106.3 0.0 collective-permute-done.13
  106.3 0.0 collective-permute-done.15
  106.3 0.1 fusion.3
  106.5 1.6 %collective-permute-done.10 = f32[4,2,64,128]{3,2,0,1:T(8,128)S(1)} collective-permute-done((f32[4,2,64,128]{3,2,0,1:T(8,128)S(1)}, f32[4,2,64,128]{3,2,0,1:T(8,128)S(1)}, u32[]{:S(2)}, u32[]{:S(2)}) %collective-permute-start.10) | collective-permute-done | bytes 262176 | tf_op jit(solution)/shard_map/ppermute | solution.py:324
  108.1 8.6 %collective-permute-done.11 = f32[4,2,64,128]{3,2,0,1:T(8,128)S(1)} collective-permute-done((f32[4,2,64,128]{3,2,0,1:T(8,128)S(1)}, f32[4,2,64,128]{3,2,0,1:T(8,128)S(1)}, u32[]{:S(2)}, u32[]{:S(2)}) %collective-permute-start.11) | collective-permute-done | bytes 262176 | tf_op jit(solution)/shard_map/ppermute | solution.py:325
  116.7 0.1 maximum_add_fusion.3
  116.7 0.1 fusion.2
  116.9 0.7 broadcast_in_dim.8
  117.6 27.9 %all-to-all-start.2 = ((f32[32,8,128]{2,1,0:T(8,128)}), f32[32,8,128]{2,1,0:T(8,128)S(1)}, u32[]{:S(2)}, u32[]{:S(2)}) async-start(f32[32,8,128]{2,1,0:T(8,128)} %broadcast_in_dim.8), calls=%async_computation.2 | async-start | bytes 262144 | tf_op jit(solution)/shard_map/all_to_all | solution.py:270
  145.5 1.1 maximum_add_fusion
  146.6 6.6 %all-to-all-done.2 = f32[32,8,128]{2,1,0:T(8,128)S(1)} async-done(((f32[32,8,128]{2,1,0:T(8,128)}), f32[32,8,128]{2,1,0:T(8,128)S(1)}, u32[]{:S(2)}, u32[]{:S(2)}) %all-to-all-start.2) | async-done | bytes 131104 | tf_op jit(solution)/shard_map/all_to_all | solution.py:270
  153.2 0.7 copy.42
  (19 shorter events, 0.4 us)
Async XLA Ops:
  2.2 7.8 %collective-permute-start.1 = (f32[4,2,64,128]{3,2,0,1:T(8,128)S(1)}, f32[4,2,64,128]{3,2,0,1:T(8,128)S(1)}, u32[]{:S(2)}, u32[]{:S(2)}) collective-permute-start(f32[4,2,64,128]{3,2,0,1:T(8,128)S(1)} %get-tuple-element.43), channel_id=1, source_target_pairs={{1,0},{2,1},{3,2},{4,3},{5,4},{6,5},{7,6},{8,7},{9,8},{10,9},{11,1... | collective-permute-start | bytes 786440 | tf_op jit(solution)/shard_map/ppermute | solution.py:286
  4.8 8.4 %collective-permute-start = (f32[4,2,64,128]{3,2,0,1:T(8,128)S(1)}, f32[4,2,64,128]{3,2,0,1:T(8,128)S(1)}, u32[]{:S(2)}, u32[]{:S(2)}) collective-permute-start(f32[4,2,64,128]{3,2,0,1:T(8,128)S(1)} %get-tuple-element.43), channel_id=1, source_target_pairs={{0,1},{1,2},{2,3},{3,4},{4,5},{5,6},{6,7},{7,8},{8,9},{9,10},{10,1... | collective-permute-start | bytes 786440 | tf_op jit(solution)/shard_map/ppermute | solution.py:285
  8.0 12.4 %collective-permute-start.4 = (f32[4,2,64,128]{3,2,1,0:T(8,128)S(1)}, f32[4,2,64,128]{3,2,1,0:T(8,128)S(1)}, u32[]{:S(2)}, u32[]{:S(2)}) collective-permute-start(f32[4,2,64,128]{3,2,1,0:T(8,128)S(1)} %pad_maximum_fusion.4), channel_id=1, source_target_pairs={{8,0},{16,8},{24,16},{40,32},{48,40},{56,48},{72,64},{80,72},{88,8... | collective-permute-start | bytes 786440 | tf_op jit(solution)/shard_map/ppermute | solution.py:247
  8.7 11.7 %collective-permute-start.2 = (f32[4,2,64,128]{3,2,1,0:T(8,128)S(1)}, f32[4,2,64,128]{3,2,1,0:T(8,128)S(1)}, u32[]{:S(2)}, u32[]{:S(2)}) collective-permute-start(f32[4,2,64,128]{3,2,1,0:T(8,128)S(1)} %pad_maximum_fusion.4), channel_id=1, source_target_pairs={{7,15},{15,23},{23,31},{39,47},{47,55},{55,63},{71,79},{79,87},{87... | collective-permute-start | bytes 786440 | tf_op jit(solution)/shard_map/ppermute | solution.py:240
  13.7 41.7 %collective-permute-start.6 = (f32[4,3,64,128]{3,2,1,0:T(8,128)S(1)}, f32[4,3,64,128]{3,2,1,0:T(8,128)S(1)}, u32[]{:S(2)}, u32[]{:S(2)}) collective-permute-start(f32[4,3,64,128]{3,2,1,0:T(8,128)S(1)} %pad_maximum_fusion.1), channel_id=1, source_target_pairs={{0,32},{32,64},{64,96},{96,128},{128,160},{160,192},{192,224},{224... | collective-permute-start | bytes 1179656 | tf_op jit(solution)/shard_map/ppermute | solution.py:290
  18.3 37.1 %copy-start.1 = (bf16[2,2,2,256,256]{4,3,2,1,0:T(8,128)(2,1)S(1)}, bf16[2,2,2,256,256]{4,3,2,1,0:T(8,128)(2,1)}, u32[]{:S(2)}) copy-start(bf16[2,2,2,256,256]{4,3,2,1,0:T(8,128)(2,1)} %constant.39.clone.table_ref) | copy-start | bytes 3145732
  18.3 37.1 %collective-permute-start.7 = (f32[4,3,64,128]{3,2,1,0:T(8,128)S(1)}, f32[4,3,64,128]{3,2,1,0:T(8,128)S(1)}, u32[]{:S(2)}, u32[]{:S(2)}) collective-permute-start(f32[4,3,64,128]{3,2,1,0:T(8,128)S(1)} %pad_maximum_fusion.2), channel_id=1, source_target_pairs={{32,0},{64,32},{96,64},{128,96},{160,128},{192,160},{224,192},{256... | collective-permute-start | bytes 1179656 | tf_op jit(solution)/shard_map/ppermute | solution.py:291
  20.6 32.4 %collective-permute-start.5 = (f32[4,2,64,128]{3,2,1,0:T(8,128)S(1)}, f32[4,2,64,128]{3,2,1,0:T(8,128)S(1)}, u32[]{:S(2)}, u32[]{:S(2)}) collective-permute-start(f32[4,2,64,128]{3,2,1,0:T(8,128)S(1)} %get-tuple-element.44), channel_id=1, source_target_pairs={{0,7},{1,0},{2,1},{3,2},{4,3},{5,4},{6,5},{7,6},{8,15},{9,8},{10,9... | collective-permute-start | bytes 786440 | tf_op jit(solution)/shard_map/ppermute | solution.py:250
  50.2 5.2 %collective-permute-start.3 = (f32[4,2,64,128]{3,2,1,0:T(8,128)S(1)}, f32[4,2,64,128]{3,2,1,0:T(8,128)S(1)}, u32[]{:S(2)}, u32[]{:S(2)}) collective-permute-start(f32[4,2,64,128]{3,2,1,0:T(8,128)S(1)} %get-tuple-element.45), channel_id=1, source_target_pairs={{0,1},{1,2},{2,3},{3,4},{4,5},{5,6},{6,7},{8,9},{9,10},{10,11},{11... | collective-permute-start | bytes 786440 | tf_op jit(solution)/shard_map/ppermute | solution.py:243
  52.2 0.7 copy-start.4
  52.9 2.5 %copy-start = (f32[4,2,64,256]{3,2,1,0:T(8,128)S(1)}, f32[4,2,64,256]{3,2,1,0:T(8,128)}, u32[]{:S(2)}) copy-start(f32[4,2,64,256]{3,2,1,0:T(8,128)} %own_ref.1) | copy-start | bytes 1572868
  52.9 2.5 %copy-start.2 = (f32[2,128,128]{2,1,0:T(8,128)S(1)}, f32[2,128,128]{2,1,0:T(8,128)}, u32[]{:S(2)}) copy-start(f32[2,128,128]{2,1,0:T(8,128)} %probe_ref.1) | copy-start | bytes 393220
  52.9 2.5 %copy-start.3 = (f32[1,1,2,128,128]{4,3,2,1,0:T(8,128)S(1)}, f32[1,1,2,128,128]{4,3,2,1,0:T(8,128)}, u32[]{:S(2)}) copy-start(f32[1,1,2,128,128]{4,3,2,1,0:T(8,128)} %param.10) | copy-start | bytes 393220
  63.0 26.8 %collective-permute-start.12 = (f32[4,2,64,128]{3,2,1,0:T(8,128)S(1)}, f32[4,2,64,128]{3,2,1,0:T(8,128)}, u32[]{:S(2)}, u32[]{:S(2)}) collective-permute-start(f32[4,2,64,128]{3,2,1,0:T(8,128)S(1)} %get-tuple-element.15), channel_id=1, source_target_pairs={{8,0},{16,8},{24,16},{40,32},{48,40},{56,48},{72,64},{80,72},{88,8... | collective-permute-start | bytes 786440 | tf_op jit(solution)/shard_map/ppermute | solution.py:247
  64.3 17.9 %all-to-all-start = ((f32[32,16,128]{2,1,0:T(8,128)}), f32[32,16,128]{2,1,0:T(8,128)S(1)}, u32[]{:S(2)}, u32[]{:S(2)}) async-start(f32[32,16,128]{2,1,0:T(8,128)} %get-tuple-element.17), calls=%async_computation | async-start | bytes 524288 | tf_op jit(solution)/shard_map/all_to_all | solution.py:270
  72.3 21.2 %collective-permute-start.14 = (f32[4,2,64,128]{3,2,1,0:T(8,128)S(1)}, f32[4,2,64,128]{3,2,1,0:T(8,128)}, u32[]{:S(2)}, u32[]{:S(2)}) collective-permute-start(f32[4,2,64,128]{3,2,1,0:T(8,128)S(1)} %get-tuple-element.16), channel_id=1, source_target_pairs={{7,15},{15,23},{23,31},{39,47},{47,55},{55,63},{71,79},{79,87},{87... | collective-permute-start | bytes 786440 | tf_op jit(solution)/shard_map/ppermute | solution.py:240
  73.7 21.9 %collective-permute-start.9 = (f32[4,3,64,128]{3,2,0,1:T(8,128)S(1)}, f32[4,3,64,128]{3,2,0,1:T(8,128)S(1)}, u32[]{:S(2)}, u32[]{:S(2)}) collective-permute-start(f32[4,3,64,128]{3,2,0,1:T(8,128)S(1)} %copy.27), channel_id=1, source_target_pairs={{32,0},{64,32},{96,64},{128,96},{160,128},{192,160},{224,192},{256... | collective-permute-start | bytes 1179656 | tf_op jit(solution)/shard_map/ppermute | solution.py:310
  77.9 20.6 %collective-permute-start.8 = (f32[4,3,64,128]{3,2,0,1:T(8,128)S(1)}, f32[4,3,64,128]{3,2,0,1:T(8,128)S(1)}, u32[]{:S(2)}, u32[]{:S(2)}) collective-permute-start(f32[4,3,64,128]{3,2,0,1:T(8,128)S(1)} %copy.26), channel_id=1, source_target_pairs={{0,32},{32,64},{64,96},{96,128},{128,160},{160,192},{192,224},{224... | collective-permute-start | bytes 1179656 | tf_op jit(solution)/shard_map/ppermute | solution.py:311
  82.9 34.0 %all-to-all-start.1 = ((f32[16,16,128]{2,1,0:T(8,128)}), f32[16,16,128]{2,1,0:T(8,128)S(1)}, u32[]{:S(2)}, u32[]{:S(2)}) async-start(f32[16,16,128]{2,1,0:T(8,128)} %broadcast_in_dim.7), calls=%async_computation.1 | async-start | bytes 262144 | tf_op jit(solution)/shard_map/all_to_all | solution.py:270
  89.9 16.4 %collective-permute-start.13 = (f32[4,2,64,128]{3,2,1,0:T(8,128)S(1)}, f32[4,2,64,128]{3,2,1,0:T(8,128)S(1)}, u32[]{:S(2)}, u32[]{:S(2)}) collective-permute-start(f32[4,2,64,128]{3,2,1,0:T(8,128)S(1)} %broadcast_select_fusion), channel_id=1, source_target_pairs={{0,7},{1,0},{2,1},{3,2},{4,3},{5,4},{6,5},{7,6},{8,15},{9,8},{10,9... | collective-permute-start | bytes 786440 | tf_op jit(solution)/shard_map/ppermute | solution.py:250
  93.5 12.8 %collective-permute-start.15 = (f32[4,2,64,128]{3,2,1,0:T(8,128)S(1)}, f32[4,2,64,128]{3,2,1,0:T(8,128)S(1)}, u32[]{:S(2)}, u32[]{:S(2)}) collective-permute-start(f32[4,2,64,128]{3,2,1,0:T(8,128)S(1)} %broadcast_select_fusion.2), channel_id=1, source_target_pairs={{0,1},{1,2},{2,3},{3,4},{4,5},{5,6},{6,7},{8,9},{9,10},{10,11},{11... | collective-permute-start | bytes 786440 | tf_op jit(solution)/shard_map/ppermute | solution.py:243
  98.9 9.2 %collective-permute-start.10 = (f32[4,2,64,128]{3,2,0,1:T(8,128)S(1)}, f32[4,2,64,128]{3,2,0,1:T(8,128)S(1)}, u32[]{:S(2)}, u32[]{:S(2)}) collective-permute-start(f32[4,2,64,128]{3,2,0,1:T(8,128)S(1)} %maximum_add_fusion.1), channel_id=1, source_target_pairs={{1,0},{2,1},{3,2},{4,3},{5,4},{6,5},{7,6},{8,7},{9,8},{10,9},{11,1... | collective-permute-start | bytes 786440 | tf_op jit(solution)/shard_map/ppermute | solution.py:324
  102.7 14.0 %collective-permute-start.11 = (f32[4,2,64,128]{3,2,0,1:T(8,128)S(1)}, f32[4,2,64,128]{3,2,0,1:T(8,128)S(1)}, u32[]{:S(2)}, u32[]{:S(2)}) collective-permute-start(f32[4,2,64,128]{3,2,0,1:T(8,128)S(1)} %maximum_add_fusion.2), channel_id=1, source_target_pairs={{0,1},{1,2},{2,3},{3,4},{4,5},{5,6},{6,7},{7,8},{8,9},{9,10},{10,1... | collective-permute-start | bytes 786440 | tf_op jit(solution)/shard_map/ppermute | solution.py:325
  117.6 35.6 %all-to-all-start.2 = ((f32[32,8,128]{2,1,0:T(8,128)}), f32[32,8,128]{2,1,0:T(8,128)S(1)}, u32[]{:S(2)}, u32[]{:S(2)}) async-start(f32[32,8,128]{2,1,0:T(8,128)} %broadcast_in_dim.8), calls=%async_computation.2 | async-start | bytes 262144 | tf_op jit(solution)/shard_map/all_to_all | solution.py:270

commit v2 on v1

v2 whole, which is shorter than its diff:
```python
import math

import jax
import jax.numpy as jnp
import ml_dtypes
import numpy as np
from jax import lax
from jax.experimental import pallas as pl
from jax.experimental.layout import Layout, with_layout_constraint
from jax.experimental.pallas import tpu as pltpu
from jax.sharding import PartitionSpec as P

distance = 0.5
SIDE = 128
HALF = 64
SLICES = 4
SLOTS = 2
RUN = 8
Z_HI, Z_LO, N_X = 4, 4, 4
VMEM_BYTES = 32 * 1024 * 1024


def split_table(matrix):
    real, imag = matrix.real, matrix.imag
    right = np.block([[real, imag], [-imag, real]]).astype(np.float32)
    parts = []
    for table in (right, right.T):
        high = table.astype(ml_dtypes.bfloat16)
        low = (table - high.astype(np.float32)).astype(ml_dtypes.bfloat16)
        parts.append(np.stack([high, low]))
    return np.stack(parts)


def tables():
    indices = np.arange(SIDE)
    fourier = np.exp(-2j * math.pi / SIDE * (np.outer(indices, indices) % SIDE)) / math.sqrt(SIDE)
    frequency = (indices + SIDE // 2) % SIDE - SIDE // 2
    phase = np.exp(-1j * math.pi * distance / SIDE * frequency * frequency)
    propagator = np.conj(fourier) @ (phase[:, None] * fourier)
    return np.stack([split_table(propagator), split_table(fourier)])


def split_value(value):
    high = value.astype(jnp.bfloat16)
    return high, (value - high.astype(jnp.float32)).astype(jnp.bfloat16)


def two_sided(fields, table_ref, which, conjugate):
    first, second = (1, 0) if conjugate else (0, 1)
    slots = len(fields)
    stacked = jnp.concatenate([jnp.concatenate(pair, axis=1) for pair in fields], axis=0)
    high, low = split_value(stacked)
    w_high, w_low = table_ref[which, first, 0], table_ref[which, first, 1]
    half = jnp.dot(
        jnp.concatenate([high, low, high], axis=1),
        jnp.concatenate([w_high, w_high, w_low], axis=0),
        preferred_element_type=jnp.float32,
    )
    rows = []
    for part in range(2):
        rows.append(
            jnp.concatenate(
                [half[k * SIDE : (k + 1) * SIDE, part * SIDE : (part + 1) * SIDE] for k in range(slots)],
                axis=1,
            )
        )
    high, low = split_value(jnp.concatenate(rows, axis=0))
    w_high, w_low = table_ref[which, second, 0], table_ref[which, second, 1]
    full = jnp.dot(
        jnp.concatenate([w_high, w_high, w_low], axis=1),
        jnp.concatenate([high, low, high], axis=0),
        preferred_element_type=jnp.float32,
    )
    return [
        (full[:SIDE, k * SIDE : (k + 1) * SIDE], full[SIDE:, k * SIDE : (k + 1) * SIDE])
        for k in range(slots)
    ]


def times(a, b):
    return (a[0] * b[0] - a[1] * b[1], a[0] * b[1] + a[1] * b[0])


def conj_times(a, b):
    return (a[0] * b[0] + a[1] * b[1], a[0] * b[1] - a[1] * b[0])


def patch_kernel(
    corner_ref,
    count_ref,
    odd_ref,
    own_ref,
    chip_ref,
    core_ref,
    chip_one_ref,
    chip_two_ref,
    own_rims_ref,
    core_rims_ref,
    probe_ref,
    measured_ref,
    table_ref,
    own_out,
    edge_out,
    mid_out,
    core_out,
    one_out,
    two_out,
    payload_out,
    extended,
    windows,
    waves,
    total,
):
    low_lanes = lax.broadcasted_iota(jnp.int32, (HALF, SIDE), 1) < HALF
    chip_row = pl.multiple_of(odd_ref[0] * 2 * HALF, HALF)
    core_row = pl.multiple_of((1 - odd_ref[0]) * 2 * HALF, HALF)
    bands = (pl.ds(chip_row, HALF), slice(HALF, 2 * HALF), pl.ds(core_row, HALF))
    odd_column = odd_ref[1] == 1
    for s in range(SLICES):
        for c in range(2):
            for b, band_ref in enumerate((chip_ref, own_ref, core_ref)):
                extended[s, c, 1, bands[b], :] = band_ref[s, c, :, :SIDE]
                extended[s, c, 2, bands[b], :] = band_ref[s, c, :, SIDE:]
        rims = (
            (chip_one_ref[s], chip_two_ref[s]),
            (own_rims_ref[0, s], own_rims_ref[1, s]),
            (core_rims_ref[0, s], core_rims_ref[1, s]),
        )
        for b, (one, two) in enumerate(rims):
            left = jnp.where(odd_column, two, one)
            right = jnp.where(odd_column, one, two)
            extended[s, 0, 0, bands[b], :] = pltpu.roll(left, HALF, 1)
            extended[s, 1, 0, bands[b], :] = left
            extended[s, 0, 3, bands[b], :] = right
            extended[s, 1, 3, bands[b], :] = pltpu.roll(right, HALF, 1)

    lanes = lax.broadcasted_iota(jnp.int32, (SIDE, SIDE), 1)
    places = []
    for k in range(SLOTS):
        row, col = corner_ref[k, 0], corner_ref[k, 1] + HALF
        places.append((row, col // SIDE, col % SIDE))
    for k in range(SLOTS):
        row, block, shift = places[k]
        back = (SIDE - shift) % SIDE
        inside = lanes < SIDE - shift
        for s in range(SLICES):
            for c in range(2):
                near = extended[s, c, block, pl.ds(row, SIDE), :]
                far = extended[s, c, block + 1, pl.ds(row, SIDE), :]
                windows[k, s, c] = jnp.where(inside, pltpu.roll(near, back, 1), pltpu.roll(far, back, 1))

    probe = (probe_ref[0], probe_ref[1])

    def layer(k, s):
        return (windows[k, s, 0], windows[k, s, 1])

    slots = range(SLOTS)
    fields = [times(probe, layer(k, 0)) for k in slots]
    for s in range(1, SLICES):
        arrived = two_sided(fields, table_ref, 0, False)
        for k in slots:
            waves[k, s - 1, 0] = arrived[k][0]
            waves[k, s - 1, 1] = arrived[k][1]
        fields = [times(arrived[k], layer(k, s)) for k in slots]
    far_fields = two_sided(fields, table_ref, 1, False)
    scaled = []
    for k in slots:
        real, imag = far_fields[k]
        residual = jnp.where(k < count_ref[0], real * real + imag * imag - measured_ref[k], 0.0)
        scaled.append((residual * real, residual * imag))
    backward = two_sided(scaled, table_ref, 1, True)

    total[...] = jnp.zeros_like(total)

    def add(k, s, pair):
        row, block, shift = places[k]
        inside = lanes >= shift
        for c in range(2):
            moved = pltpu.roll(pair[c], shift, 1)
            total[s, c, block, pl.ds(row, SIDE), :] += jnp.where(inside, moved, 0.0)
            total[s, c, block + 1, pl.ds(row, SIDE), :] += jnp.where(inside, 0.0, moved)

    for s in range(SLICES - 1, 0, -1):
        for k in slots:
            add(k, s, conj_times((waves[k, s - 1, 0], waves[k, s - 1, 1]), backward[k]))
        backward = two_sided([conj_times(layer(k, s), backward[k]) for k in slots], table_ref, 0, True)
    for k in slots:
        add(k, 0, conj_times(probe, backward[k]))
    terms = [conj_times(layer(k, 0), backward[k]) for k in slots]
    for c in range(2):
        summed = (terms[0][c] + terms[1][c]).reshape(16, 8, SIDE)
        payload_out[c * 16 : (c + 1) * 16, 0:8, :] = summed
    payload_out[:, 8:16, :] = jnp.full((32, 8, SIDE), count_ref[0].astype(jnp.float32), jnp.float32)

    for s in range(SLICES):
        for c in range(2):
            first, second = total[s, c, 1, bands[0], :], total[s, c, 2, bands[0], :]
            edge_out[s, c] = jnp.where(low_lanes, first, second)
            mid_out[s, c] = jnp.where(low_lanes, second, first)
            for b, band_out in ((1, own_out), (2, core_out)):
                band_out[s, c, :, :SIDE] = total[s, c, 1, bands[b], :]
                band_out[s, c, :, SIDE:] = total[s, c, 2, bands[b], :]
        for b in range(3):
            left = jnp.where(
                low_lanes, pltpu.roll(total[s, 0, 0, bands[b], :], HALF, 1), total[s, 1, 0, bands[b], :]
            )
            right = jnp.where(
                low_lanes, total[s, 0, 3, bands[b], :], pltpu.roll(total[s, 1, 3, bands[b], :], HALF, 1)
            )
            one_out[s, b] = jnp.where(odd_column, right, left)
            two_out[s, b] = jnp.where(odd_column, left, right)


def gradients(*operands):
    f32 = jnp.float32
    rim = jax.ShapeDtypeStruct((SLICES, 3, HALF, SIDE), f32)

    def band(width):
        return jax.ShapeDtypeStruct((SLICES, 2, HALF, width), f32)

    shapes = [
        band(2 * SIDE),
        band(SIDE),
        band(SIDE),
        band(2 * SIDE),
        rim,
        rim,
        jax.ShapeDtypeStruct((32, 16, SIDE), f32),
    ]

    def whole(array):
        return pl.BlockSpec(array.shape, lambda i, zeros=(0,) * len(array.shape): zeros)

    smem = pl.BlockSpec(memory_space=pltpu.SMEM)
    return pl.pallas_call(
        patch_kernel,
        grid=(1,),
        out_shape=shapes,
        in_specs=[smem] * 3 + [whole(array) for array in operands[3:]],
        out_specs=[whole(array) for array in shapes],
        scratch_shapes=[
            pltpu.VMEM((SLICES, 2, 4, 3 * HALF, SIDE), f32),
            pltpu.VMEM((SLOTS, SLICES, 2, SIDE, SIDE), f32),
            pltpu.VMEM((SLOTS, SLICES - 1, 2, SIDE, SIDE), f32),
            pltpu.VMEM((SLICES, 2, 4, 3 * HALF, SIDE), f32),
        ],
        compiler_params=pltpu.CompilerParams(vmem_limit_bytes=VMEM_BYTES),
    )(*operands)


def pack(field):
    return jnp.concatenate([field[:, 0], field[:, 1]], axis=-1)


def unpack(field):
    return jnp.stack([field[..., :HALF], field[..., HALF:]], axis=1)


def near_groups():
    return [
        [(x * Z_LO + low) * Z_HI * RUN + high * RUN + m for x in range(N_X) for m in range(RUN)]
        for low in range(Z_LO)
        for high in range(Z_HI)
    ]


def far_groups():
    return [
        [(x * Z_LO + low) * Z_HI * RUN + high * RUN + m for high in range(Z_HI) for low in range(Z_LO)]
        for x in range(N_X)
        for m in range(RUN)
    ]


def exchange(pieces, groups):
    return lax.all_to_all(pieces, ("gx", "gy"), 0, 0, tiled=True, axis_index_groups=groups)


def plain(array):
    return with_layout_constraint(array, Layout(major_to_minor=tuple(range(array.ndim))))


def partners(axis, first):
    count = lax.axis_size(axis)
    both = [(i, i + 1) for i in range(first, count - 1, 2)]
    return both + [(j, i) for i, j in both]


def body(object_slices, probe, positions, counts, measured):
    cols = object_slices.shape[3]
    row, col = lax.axis_index("gy"), lax.axis_index("gx")
    odd_column = col % 2 == 1
    chips, cores = partners("gy", 1), partners("gy", 0)
    ones, twos = partners("gx", 1), partners("gx", 0)
    rows = lax.axis_size("gy")
    hops = [(i, i + RUN) for i in range(RUN - 1, rows - RUN, RUN)] + [(i, i - RUN) for i in range(RUN, rows, RUN)]
    turns = [(i, j) for i, j in chips if i // RUN == j // RUN]
    turns += [(i + RUN - 1, i) for i in range(RUN, rows, RUN)] + [(i, i + RUN - 1) for i in range(0, rows - RUN, RUN)]
    odd = jnp.stack([row % 2, col % 2]).astype(jnp.int32)

    def swap(first, second):
        return lax.ppermute(first, "gx", ones), lax.ppermute(second, "gx", twos)

    def sides(band):
        left, right = pack(band[..., :HALF]), pack(band[..., cols - HALF :])
        return jnp.where(odd_column, right, left), jnp.where(odd_column, left, right)

    chip_band = plain(lax.ppermute(plain(object_slices), "gy", chips))
    core_band = plain(lax.ppermute(plain(object_slices), "gy", cores))
    own_rims = jnp.stack(swap(*sides(object_slices)))
    corners = positions[0, 0] - jnp.stack([row * HALF, col * cols]).astype(jnp.int32)[None, :] + HALF
    chip_band, own_rims, corners, odd = lax.optimization_barrier((chip_band, own_rims, corners, odd))
    core_rims = lax.ppermute(own_rims, "gy", cores)
    chip_one, chip_two = swap(*sides(chip_band))

    own, edge, mid, to_core, one, two, payload = gradients(
        corners,
        counts[0],
        odd,
        object_slices,
        chip_band,
        core_band,
        chip_one,
        chip_two,
        own_rims,
        core_rims,
        probe,
        measured[0, 0],
        jnp.asarray(tables()),
    )

    def columns(one, two):
        return unpack(jnp.where(odd_column, two, one)), unpack(jnp.where(odd_column, one, two))

    def with_rims(band, one, two):
        left, right = columns(one, two)
        middle = jnp.zeros(band.shape[:3] + (cols - 2 * HALF,), band.dtype)
        return band + jnp.concatenate([left, middle, right], axis=3)

    near, far = near_groups(), far_groups()
    at_end = (row % RUN == 0) | (row % RUN == RUN - 1)
    far_mid = plain(lax.ppermute(plain(mid), "gy", hops))
    mid = plain(lax.ppermute(plain(jnp.where(at_end, far_mid, mid)), "gy", turns))
    one, two = swap(plain(one), plain(two))
    one, two = plain(one), plain(two)
    part = jnp.sum(exchange(payload, near), axis=0)
    edge = edge + jnp.concatenate(columns(one[:, 0], two[:, 0]), axis=3)
    to_core = with_rims(to_core, one[:, 2], two[:, 2])
    edge = plain(lax.ppermute(plain(edge), "gy", chips))
    part = jnp.sum(exchange(jnp.broadcast_to(part, (Z_LO * Z_HI, 16, SIDE)), far), axis=0)
    part = part[:8] / part[8:]
    from_core = plain(lax.ppermute(plain(to_core), "gy", cores))
    probe_grad = exchange(jnp.broadcast_to(part, (32, 8, SIDE)), near).reshape(2, SIDE, SIDE)
    from_chip = jnp.concatenate([edge[..., :HALF], mid[..., HALF:], mid[..., :HALF], edge[..., HALF:]], axis=3)
    return plain(with_rims(own, one[:, 1], two[:, 1]) + from_core + from_chip), probe_grad


def solution(mesh):
    placed = (
        P(None, None, "gy", "gx"),
        P(),
        P("gy", "gx", None, None),
        P("gy", "gx"),
        P("gy", "gx", None, None, None),
    )
    return jax.shard_map(
        body,
        mesh=mesh,
        in_specs=placed,
        out_specs=(P(None, None, "gy", "gx"), P()),
        check_vma=False,
    )
```

time: 155 us -> 132 us (0.85)
  the two profiles are of different devices: /device:TPU:481 before, /device:TPU:1 now
where the time goes in v2:
time: 132 us; the launch traced here: 131 us
  starting transfers between devices  85 us (64%)
  waiting for transfers between devices  29.6 us (22%)
  Pallas kernels  7.55 us (6%)
  local copies, waits for them, and re-layouts  4.79 us (4%)
  other arithmetic  2.87 us (2%)
  between operations  1.7 us (1%)
    all_to_all x3, starting transfers between devices, exchange(): lax.all_to_all(pieces, ('gx', 'gy'), 0, 0, tiled=True, axis_index_groups=...  44.3 us
    all_to_all x3, waiting for transfers between devices, exchange(): lax.all_to_all(pieces, ('gx', 'gy'), 0, 0, tiled=True, axis_index_groups=...  19.3 us
    ppermute x6, starting transfers between devices, swap(): return (lax.ppermute(first, 'gx', ones), lax.ppermute(second, 'gx', twos))  19.1 us
    ppermute x6, waiting for transfers between devices, swap(): return (lax.ppermute(first, 'gx', ones), lax.ppermute(second, 'gx', twos))  10.2 us
    pallas_call x1, Pallas kernels, gradients(): pl.pallas_call(patch_kernel, grid=(1,), out_shape=shapes, in_specs=[smem]...  7.55 us
    ppermute x1, starting transfers between devices, body(): core_band = plain(lax.ppermute(plain(object_slices), 'gy', cores))  4.89 us
    ppermute x1, starting transfers between devices, body(): chip_band = plain(lax.ppermute(plain(object_slices), 'gy', chips))  4.6 us
    ppermute x1, starting transfers between devices, body(): edge = plain(lax.ppermute(plain(edge), 'gy', chips))  3.39 us
  transfers between devices with their start and end apart: 16, of which 5 were waited for; matrix products, arithmetic and copies ran while one was open for 4% of the time, Pallas kernels for 0%

profile of v2, /device:TPU:1, one launch (start us, length us, event | category | flops | bytes accessed | tf_op | source)
XLA Modules:
  0.0 131.4 jit_solution(14327658656471034339)
XLA Ops:
  0.6 4.6 %collective-permute-start = (f32[4,2,64,256]{3,2,1,0:T(8,128)}, f32[4,2,64,256]{3,2,1,0:T(8,128)S(1)}, u32[]{:S(2)}, u32[]{:S(2)}) collective-permute-start(f32[4,2,64,256]{3,2,1,0:T(8,128)} %own_ref.1), channel_id=1, source_target_pairs={{1,2},{3,4},{5,6},{7,8},{9,10},{11,12},{13,14},{15,16},{17,18},{19... | collective-permute-start | bytes 1572872 | tf_op jit(solution)/shard_map/ppermute | solution.py:308
  5.2 4.9 %collective-permute-start.3 = (f32[4,2,64,256]{3,2,1,0:T(8,128)}, f32[4,2,64,256]{3,2,1,0:T(8,128)S(1)}, u32[]{:S(2)}, u32[]{:S(2)}) collective-permute-start(f32[4,2,64,256]{3,2,1,0:T(8,128)} %own_ref.1), channel_id=1, source_target_pairs={{0,1},{2,3},{4,5},{6,7},{8,9},{10,11},{12,13},{14,15},{16,17},{18,... | collective-permute-start | bytes 1572872 | tf_op jit(solution)/shard_map/ppermute | solution.py:309
  10.1 1.2 slice_bitcast_fusion.25
  11.4 0.1 broadcast_select_fusion.4
  11.5 0.7 collective-permute-start.1
  12.2 3.5 %collective-permute-start.2 = (f32[4,64,128]{2,1,0:T(8,128)S(1)}, f32[4,64,128]{2,1,0:T(8,128)S(1)}, u32[]{:S(2)}, u32[]{:S(2)}) collective-permute-start(f32[4,64,128]{2,1,0:T(8,128)S(1)} %get-tuple-element.37), channel_id=1, source_target_pairs={{0,32},{64,96},{128,160},{192,224},{256,288},{320,352},{384,416},{... | collective-permute-start | bytes 393224 | tf_op jit(solution)/shard_map/ppermute | solution.py:302
  15.7 0.0 copy-start.4
  15.7 0.1 pad_add_fusion
  15.8 0.6 copy-done.4
  16.4 0.1 pad_add_fusion.1.odd_ref
  16.5 0.0 collective-permute-done.1
  16.5 6.6 %collective-permute-done.2 = f32[4,64,128]{2,1,0:T(8,128)S(1)} collective-permute-done((f32[4,64,128]{2,1,0:T(8,128)S(1)}, f32[4,64,128]{2,1,0:T(8,128)S(1)}, u32[]{:S(2)}, u32[]{:S(2)}) %collective-permute-start.2) | collective-permute-done | bytes 131104 | tf_op jit(solution)/shard_map/ppermute | solution.py:302
  23.1 0.0 copy-start.1
  23.1 0.0 collective-permute-done.chip_ref
  23.1 3.2 %collective-permute-start.6 = (f32[2,4,64,128]{3,2,1,0:T(8,128)S(1)}, f32[2,4,64,128]{3,2,1,0:T(8,128)S(1)}, u32[]{:S(2)}, u32[]{:S(2)}) collective-permute-start(f32[2,4,64,128]{3,2,1,0:T(8,128)S(1)} %pad_maximum_fusion.own_rims_ref), channel_id=1, source_target_pairs={{0,1},{2,3},{4,5},{6,7},{8,9},{10,11},{12,13},{14,15},{16,17},{18,... | collective-permute-start | bytes 786440 | tf_op jit(solution)/shard_map/ppermute | solution.py:313
  26.3 0.1 slice_bitcast_fusion.21
  26.4 0.0 copy-start
  26.4 0.0 copy-start.2
  26.5 0.0 copy-start.3
  26.5 0.1 broadcast_select_fusion.1
  26.6 0.8 collective-permute-start.4
  27.4 10.9 %collective-permute-start.5 = (f32[4,64,128]{2,1,0:T(8,128)S(1)}, f32[4,64,128]{2,1,0:T(8,128)S(1)}, u32[]{:S(2)}, u32[]{:S(2)}) collective-permute-start(f32[4,64,128]{2,1,0:T(8,128)S(1)} %get-tuple-element.30), channel_id=1, source_target_pairs={{0,32},{64,96},{128,160},{192,224},{256,288},{320,352},{384,416},{... | collective-permute-start | bytes 393224 | tf_op jit(solution)/shard_map/ppermute | solution.py:302
  39.0 0.0 collective-permute-done.3.core_ref
  39.0 0.0 collective-permute-done.4.chip_one_ref
  39.0 3.6 %collective-permute-done.5.chip_two_ref = f32[4,64,128]{2,1,0:T(8,128)S(1)} collective-permute-done((f32[4,64,128]{2,1,0:T(8,128)S(1)}, f32[4,64,128]{2,1,0:T(8,128)S(1)}, u32[]{:S(2)}, u32[]{:S(2)}) %collective-permute-start.5) | collective-permute-done | bytes 131104 | tf_op jit(solution)/shard_map/ppermute | solution.py:302
  42.6 0.0 collective-permute-done.6.core_rims_ref
  42.6 0.0 copy-done.1
  42.6 0.0 copy-done
  42.6 0.0 copy-done.2
  42.7 0.0 copy-done.3
  42.7 7.6 %shard_map.77 = (f32[4,2,64,256]{3,2,1,0:T(8,128)S(1)}, f32[4,2,64,128]{3,2,1,0:T(8,128)S(1)}, f32[4,2,64,128]{3,2,1,0:T(8,128)S(1)}, f32[4,2,64,256]{3,2,1,0:T(...) custom-call(s32[2,2]{1,0:T(2,128)S(1)} %fusion.2.corner_ref, ...), custom_call_target="tpu_custom_call" | custom-call | tf_op jit(solution)/shard_map/pallas_call | solution.py:235
  50.2 1.4 %collective-permute-start.11 = (f32[4,2,64,128]{3,2,1,0:T(8,128)S(1)}, f32[4,2,64,128]{3,2,1,0:T(8,128)}, u32[]{:S(2)}, u32[]{:S(2)}) collective-permute-start(f32[4,2,64,128]{3,2,1,0:T(8,128)S(1)} %get-tuple-element.22), channel_id=1, source_target_pairs={{7,15},{15,23},{23,31},{8,0},{16,8},{24,16},{39,47},{47,55},{55,63... | collective-permute-start | bytes 786440 | tf_op jit(solution)/shard_map/ppermute | solution.py:342
  51.6 26.1 %all-to-all-start = ((f32[32,16,128]{2,1,0:T(8,128)}), f32[32,16,128]{2,1,0:T(8,128)S(1)}, u32[]{:S(2)}, u32[]{:S(2)}) async-start(f32[32,16,128]{2,1,0:T(8,128)} %get-tuple-element.23), calls=%async_computation | async-start | bytes 524288 | tf_op jit(solution)/shard_map/all_to_all | solution.py:276
  77.7 2.6 %collective-permute-start.7 = (f32[4,3,64,128]{3,2,1,0:T(8,128)S(1)}, f32[4,3,64,128]{3,2,1,0:T(8,128)S(1)}, u32[]{:S(2)}, u32[]{:S(2)}) collective-permute-start(f32[4,3,64,128]{3,2,1,0:T(8,128)S(1)} %get-tuple-element.18), channel_id=1, source_target_pairs={{0,32},{64,96},{128,160},{192,224},{256,288},{320,352},{384,416},{... | collective-permute-start | bytes 1179656 | tf_op jit(solution)/shard_map/ppermute | solution.py:302
  80.3 0.7 collective-permute-start.8
  81.1 0.1 pad.16.clone
  81.1 5.6 %all-to-all-done = f32[32,16,128]{2,1,0:T(8,128)S(1)} async-done(((f32[32,16,128]{2,1,0:T(8,128)}), f32[32,16,128]{2,1,0:T(8,128)S(1)}, u32[]{:S(2)}, u32[]{:S(2)}) %all-to-all-start) | async-done | bytes 262176 | tf_op jit(solution)/shard_map/all_to_all | solution.py:276
  86.8 0.7 broadcast_in_dim.7
  87.4 6.2 %all-to-all-start.1 = ((f32[16,16,128]{2,1,0:T(8,128)}), f32[16,16,128]{2,1,0:T(8,128)S(1)}, u32[]{:S(2)}, u32[]{:S(2)}) async-start(f32[16,16,128]{2,1,0:T(8,128)} %broadcast_in_dim.7), calls=%async_computation.1 | async-start | bytes 262144 | tf_op jit(solution)/shard_map/all_to_all | solution.py:276
  93.6 0.0 collective-permute-done.11
  93.7 2.2 %collective-permute-start.12 = (f32[4,2,64,128]{3,2,1,0:T(8,128)S(1)}, f32[4,2,64,128]{3,2,1,0:T(8,128)S(1)}, u32[]{:S(2)}, u32[]{:S(2)}) collective-permute-start(f32[4,2,64,128]{3,2,1,0:T(8,128)S(1)} %broadcast_select_fusion), channel_id=1, source_target_pairs={{1,2},{3,4},{5,6},{9,10},{11,12},{13,14},{17,18},{19,20},{21,22},{... | collective-permute-start | bytes 786440 | tf_op jit(solution)/shard_map/ppermute | solution.py:343
  95.9 0.0 collective-permute-done.7
  95.9 0.0 collective-permute-done.8
  95.9 0.1 select_bitcast_fusion.1
  96.0 0.1 slice_bitcast_fusion.1
  96.1 0.1 maximum_add_fusion.2
  96.3 3.4 %collective-permute-start.10 = (f32[4,2,64,128]{3,2,1,0:T(8,128)S(1)}, f32[4,2,64,128]{3,2,1,0:T(8,128)S(1)}, u32[]{:S(2)}, u32[]{:S(2)}) collective-permute-start(f32[4,2,64,128]{3,2,1,0:T(8,128)S(1)} %copy.47), channel_id=1, source_target_pairs={{1,2},{3,4},{5,6},{7,8},{9,10},{11,12},{13,14},{15,16},{17,18},{19... | collective-permute-start | bytes 786440 | tf_op jit(solution)/shard_map/ppermute | solution.py:349
  99.7 0.1 slice_bitcast_fusion.7
  99.9 0.9 maximum_add_fusion.1
  100.8 1.9 %collective-permute-start.9 = (f32[4,2,64,256]{3,2,1,0:T(8,128)}, f32[4,2,64,256]{3,2,1,0:T(8,128)S(1)}, u32[]{:S(2)}, u32[]{:S(2)}) collective-permute-start(f32[4,2,64,256]{3,2,1,0:T(8,128)} %maximum_add_fusion.1), channel_id=1, source_target_pairs={{0,1},{2,3},{4,5},{6,7},{8,9},{10,11},{12,13},{14,15},{16,17},{18,... | collective-permute-start | bytes 1572872 | tf_op jit(solution)/shard_map/ppermute | solution.py:352
  102.7 0.1 slice_bitcast_fusion.15
  102.8 0.1 slice_bitcast_fusion.13
  102.9 0.0 collective-permute-done.12
  102.9 0.1 fusion.4
  103.1 6.2 %all-to-all-done.1 = f32[16,16,128]{2,1,0:T(8,128)S(1)} async-done(((f32[16,16,128]{2,1,0:T(8,128)}), f32[16,16,128]{2,1,0:T(8,128)S(1)}, u32[]{:S(2)}, u32[]{:S(2)}) %all-to-all-start.1) | async-done | bytes 131104 | tf_op jit(solution)/shard_map/all_to_all | solution.py:276
  109.3 0.7 broadcast_in_dim.8
  109.9 12.0 %all-to-all-start.2 = ((f32[32,8,128]{2,1,0:T(8,128)}), f32[32,8,128]{2,1,0:T(8,128)S(1)}, u32[]{:S(2)}, u32[]{:S(2)}) async-start(f32[32,8,128]{2,1,0:T(8,128)} %broadcast_in_dim.8), calls=%async_computation.2 | async-start | bytes 262144 | tf_op jit(solution)/shard_map/all_to_all | solution.py:276
  121.9 0.0 collective-permute-done.10
  122.0 0.1 fusion.3
  122.1 7.6 %all-to-all-done.2 = f32[32,8,128]{2,1,0:T(8,128)S(1)} async-done(((f32[32,8,128]{2,1,0:T(8,128)}), f32[32,8,128]{2,1,0:T(8,128)S(1)}, u32[]{:S(2)}, u32[]{:S(2)}) %all-to-all-start.2) | async-done | bytes 131104 | tf_op jit(solution)/shard_map/all_to_all | solution.py:276
  129.6 0.0 collective-permute-done.9
  129.6 1.1 fusion.1
  130.8 0.7 copy.69
  (9 shorter events, 0.2 us)
Async XLA Ops:
  0.6 22.5 %collective-permute-start = (f32[4,2,64,256]{3,2,1,0:T(8,128)}, f32[4,2,64,256]{3,2,1,0:T(8,128)S(1)}, u32[]{:S(2)}, u32[]{:S(2)}) collective-permute-start(f32[4,2,64,256]{3,2,1,0:T(8,128)} %own_ref.1), channel_id=1, source_target_pairs={{1,2},{3,4},{5,6},{7,8},{9,10},{11,12},{13,14},{15,16},{17,18},{19... | collective-permute-start | bytes 1572872 | tf_op jit(solution)/shard_map/ppermute | solution.py:308
  5.2 33.8 %collective-permute-start.3 = (f32[4,2,64,256]{3,2,1,0:T(8,128)}, f32[4,2,64,256]{3,2,1,0:T(8,128)S(1)}, u32[]{:S(2)}, u32[]{:S(2)}) collective-permute-start(f32[4,2,64,256]{3,2,1,0:T(8,128)} %own_ref.1), channel_id=1, source_target_pairs={{0,1},{2,3},{4,5},{6,7},{8,9},{10,11},{12,13},{14,15},{16,17},{18,... | collective-permute-start | bytes 1572872 | tf_op jit(solution)/shard_map/ppermute | solution.py:309
  11.5 4.9 %collective-permute-start.1 = (f32[4,64,128]{2,1,0:T(8,128)S(1)}, f32[4,64,128]{2,1,0:T(8,128)S(1)}, u32[]{:S(2)}, u32[]{:S(2)}) collective-permute-start(f32[4,64,128]{2,1,0:T(8,128)S(1)} %get-tuple-element.36), channel_id=1, source_target_pairs={{32,64},{96,128},{160,192},{224,256},{288,320},{352,384},{416,448}... | collective-permute-start | bytes 393224 | tf_op jit(solution)/shard_map/ppermute | solution.py:302
  12.2 10.8 %collective-permute-start.2 = (f32[4,64,128]{2,1,0:T(8,128)S(1)}, f32[4,64,128]{2,1,0:T(8,128)S(1)}, u32[]{:S(2)}, u32[]{:S(2)}) collective-permute-start(f32[4,64,128]{2,1,0:T(8,128)S(1)} %get-tuple-element.37), channel_id=1, source_target_pairs={{0,32},{64,96},{128,160},{192,224},{256,288},{320,352},{384,416},{... | collective-permute-start | bytes 393224 | tf_op jit(solution)/shard_map/ppermute | solution.py:302
  15.7 0.7 copy-start.4
  23.1 19.6 %copy-start.1 = (bf16[2,2,2,256,256]{4,3,2,1,0:T(8,128)(2,1)S(1)}, bf16[2,2,2,256,256]{4,3,2,1,0:T(8,128)(2,1)}, u32[]{:S(2)}) copy-start(bf16[2,2,2,256,256]{4,3,2,1,0:T(8,128)(2,1)} %constant.53.clone.table_ref) | copy-start | bytes 3145732
  23.1 19.5 %collective-permute-start.6 = (f32[2,4,64,128]{3,2,1,0:T(8,128)S(1)}, f32[2,4,64,128]{3,2,1,0:T(8,128)S(1)}, u32[]{:S(2)}, u32[]{:S(2)}) collective-permute-start(f32[2,4,64,128]{3,2,1,0:T(8,128)S(1)} %pad_maximum_fusion.own_rims_ref), channel_id=1, source_target_pairs={{0,1},{2,3},{4,5},{6,7},{8,9},{10,11},{12,13},{14,15},{16,17},{18,... | collective-permute-start | bytes 786440 | tf_op jit(solution)/shard_map/ppermute | solution.py:313
  26.4 16.2 %copy-start = (f32[4,2,64,256]{3,2,1,0:T(8,128)S(1)}, f32[4,2,64,256]{3,2,1,0:T(8,128)}, u32[]{:S(2)}) copy-start(f32[4,2,64,256]{3,2,1,0:T(8,128)} %own_ref.1) | copy-start | bytes 1572868
  26.4 16.2 %copy-start.2 = (f32[2,128,128]{2,1,0:T(8,128)S(1)}, f32[2,128,128]{2,1,0:T(8,128)}, u32[]{:S(2)}) copy-start(f32[2,128,128]{2,1,0:T(8,128)} %probe_ref.1) | copy-start | bytes 393220
  26.5 16.2 %copy-start.3 = (f32[1,1,2,128,128]{4,3,2,1,0:T(8,128)S(1)}, f32[1,1,2,128,128]{4,3,2,1,0:T(8,128)}, u32[]{:S(2)}) copy-start(f32[1,1,2,128,128]{4,3,2,1,0:T(8,128)} %param.10) | copy-start | bytes 393220
  26.6 12.4 %collective-permute-start.4 = (f32[4,64,128]{2,1,0:T(8,128)S(1)}, f32[4,64,128]{2,1,0:T(8,128)S(1)}, u32[]{:S(2)}, u32[]{:S(2)}) collective-permute-start(f32[4,64,128]{2,1,0:T(8,128)S(1)} %get-tuple-element.31), channel_id=1, source_target_pairs={{32,64},{96,128},{160,192},{224,256},{288,320},{352,384},{416,448}... | collective-permute-start | bytes 393224 | tf_op jit(solution)/shard_map/ppermute | solution.py:302
  27.4 15.2 %collective-permute-start.5 = (f32[4,64,128]{2,1,0:T(8,128)S(1)}, f32[4,64,128]{2,1,0:T(8,128)S(1)}, u32[]{:S(2)}, u32[]{:S(2)}) collective-permute-start(f32[4,64,128]{2,1,0:T(8,128)S(1)} %get-tuple-element.30), channel_id=1, source_target_pairs={{0,32},{64,96},{128,160},{192,224},{256,288},{320,352},{384,416},{... | collective-permute-start | bytes 393224 | tf_op jit(solution)/shard_map/ppermute | solution.py:302
  50.2 43.4 %collective-permute-start.11 = (f32[4,2,64,128]{3,2,1,0:T(8,128)S(1)}, f32[4,2,64,128]{3,2,1,0:T(8,128)}, u32[]{:S(2)}, u32[]{:S(2)}) collective-permute-start(f32[4,2,64,128]{3,2,1,0:T(8,128)S(1)} %get-tuple-element.22), channel_id=1, source_target_pairs={{7,15},{15,23},{23,31},{8,0},{16,8},{24,16},{39,47},{47,55},{55,63... | collective-permute-start | bytes 786440 | tf_op jit(solution)/shard_map/ppermute | solution.py:342
  51.6 35.1 %all-to-all-start = ((f32[32,16,128]{2,1,0:T(8,128)}), f32[32,16,128]{2,1,0:T(8,128)S(1)}, u32[]{:S(2)}, u32[]{:S(2)}) async-start(f32[32,16,128]{2,1,0:T(8,128)} %get-tuple-element.23), calls=%async_computation | async-start | bytes 524288 | tf_op jit(solution)/shard_map/all_to_all | solution.py:276
  77.7 18.1 %collective-permute-start.7 = (f32[4,3,64,128]{3,2,1,0:T(8,128)S(1)}, f32[4,3,64,128]{3,2,1,0:T(8,128)S(1)}, u32[]{:S(2)}, u32[]{:S(2)}) collective-permute-start(f32[4,3,64,128]{3,2,1,0:T(8,128)S(1)} %get-tuple-element.18), channel_id=1, source_target_pairs={{0,32},{64,96},{128,160},{192,224},{256,288},{320,352},{384,416},{... | collective-permute-start | bytes 1179656 | tf_op jit(solution)/shard_map/ppermute | solution.py:302
  80.3 15.5 %collective-permute-start.8 = (f32[4,3,64,128]{3,2,1,0:T(8,128)S(1)}, f32[4,3,64,128]{3,2,1,0:T(8,128)S(1)}, u32[]{:S(2)}, u32[]{:S(2)}) collective-permute-start(f32[4,3,64,128]{3,2,1,0:T(8,128)S(1)} %get-tuple-element.19), channel_id=1, source_target_pairs={{32,64},{96,128},{160,192},{224,256},{288,320},{352,384},{416,448}... | collective-permute-start | bytes 1179656 | tf_op jit(solution)/shard_map/ppermute | solution.py:302
  87.4 21.8 %all-to-all-start.1 = ((f32[16,16,128]{2,1,0:T(8,128)}), f32[16,16,128]{2,1,0:T(8,128)S(1)}, u32[]{:S(2)}, u32[]{:S(2)}) async-start(f32[16,16,128]{2,1,0:T(8,128)} %broadcast_in_dim.7), calls=%async_computation.1 | async-start | bytes 262144 | tf_op jit(solution)/shard_map/all_to_all | solution.py:276
  93.7 9.2 %collective-permute-start.12 = (f32[4,2,64,128]{3,2,1,0:T(8,128)S(1)}, f32[4,2,64,128]{3,2,1,0:T(8,128)S(1)}, u32[]{:S(2)}, u32[]{:S(2)}) collective-permute-start(f32[4,2,64,128]{3,2,1,0:T(8,128)S(1)} %broadcast_select_fusion), channel_id=1, source_target_pairs={{1,2},{3,4},{5,6},{9,10},{11,12},{13,14},{17,18},{19,20},{21,22},{... | collective-permute-start | bytes 786440 | tf_op jit(solution)/shard_map/ppermute | solution.py:343
  96.3 25.7 %collective-permute-start.10 = (f32[4,2,64,128]{3,2,1,0:T(8,128)S(1)}, f32[4,2,64,128]{3,2,1,0:T(8,128)S(1)}, u32[]{:S(2)}, u32[]{:S(2)}) collective-permute-start(f32[4,2,64,128]{3,2,1,0:T(8,128)S(1)} %copy.47), channel_id=1, source_target_pairs={{1,2},{3,4},{5,6},{7,8},{9,10},{11,12},{13,14},{15,16},{17,18},{19... | collective-permute-start | bytes 786440 | tf_op jit(solution)/shard_map/ppermute | solution.py:349
  100.8 28.9 %collective-permute-start.9 = (f32[4,2,64,256]{3,2,1,0:T(8,128)}, f32[4,2,64,256]{3,2,1,0:T(8,128)S(1)}, u32[]{:S(2)}, u32[]{:S(2)}) collective-permute-start(f32[4,2,64,256]{3,2,1,0:T(8,128)} %maximum_add_fusion.1), channel_id=1, source_target_pairs={{0,1},{2,3},{4,5},{6,7},{8,9},{10,11},{12,13},{14,15},{16,17},{18,... | collective-permute-start | bytes 1572872 | tf_op jit(solution)/shard_map/ppermute | solution.py:352
  109.9 19.7 %all-to-all-start.2 = ((f32[32,8,128]{2,1,0:T(8,128)}), f32[32,8,128]{2,1,0:T(8,128)S(1)}, u32[]{:S(2)}, u32[]{:S(2)}) async-start(f32[32,8,128]{2,1,0:T(8,128)} %broadcast_in_dim.8), calls=%async_computation.2 | async-start | bytes 262144 | tf_op jit(solution)/shard_map/all_to_all | solution.py:276

commit v3 on v2

--- a/solution.py
+++ b/solution.py
@@ -309,8 +309,8 @@
     core_band = plain(lax.ppermute(plain(object_slices), "gy", cores))
     own_rims = jnp.stack(swap(*sides(object_slices)))
     corners = positions[0, 0] - jnp.stack([row * HALF, col * cols]).astype(jnp.int32)[None, :] + HALF
+    core_rims = plain(lax.ppermute(plain(own_rims), "gy", cores))
     chip_band, own_rims, corners, odd = lax.optimization_barrier((chip_band, own_rims, corners, odd))
-    core_rims = lax.ppermute(own_rims, "gy", cores)
     chip_one, chip_two = swap(*sides(chip_band))
 
     own, edge, mid, to_core, one, two, payload = gradients(

time: 132 us -> 132 us (level)
  no operation moved by 1% of the time
where the time goes in v3:
time: 132 us; the launch traced here: 131 us
  starting transfers between devices  84.4 us (64%)
  waiting for transfers between devices  29.7 us (22%)
  Pallas kernels  7.57 us (6%)
  local copies, waits for them, and re-layouts  4.79 us (4%)
  other arithmetic  2.87 us (2%)
  between operations  1.7 us (1%)
    all_to_all x3, starting transfers between devices, exchange(): lax.all_to_all(pieces, ('gx', 'gy'), 0, 0, tiled=True, axis_index_groups=...  43.8 us
    all_to_all x3, waiting for transfers between devices, exchange(): lax.all_to_all(pieces, ('gx', 'gy'), 0, 0, tiled=True, axis_index_groups=...  19.4 us
    ppermute x6, starting transfers between devices, swap(): return (lax.ppermute(first, 'gx', ones), lax.ppermute(second, 'gx', twos))  19.1 us
    ppermute x6, waiting for transfers between devices, swap(): return (lax.ppermute(first, 'gx', ones), lax.ppermute(second, 'gx', twos))  10.2 us
    pallas_call x1, Pallas kernels, gradients(): pl.pallas_call(patch_kernel, grid=(1,), out_shape=shapes, in_specs=[smem]...  7.57 us
    ppermute x1, starting transfers between devices, body(): core_band = plain(lax.ppermute(plain(object_slices), 'gy', cores))  4.89 us
    ppermute x1, starting transfers between devices, body(): chip_band = plain(lax.ppermute(plain(object_slices), 'gy', chips))  4.6 us
    ppermute x1, starting transfers between devices, body(): edge = plain(lax.ppermute(plain(edge), 'gy', chips))  3.39 us
  transfers between devices with their start and end apart: 16, of which 5 were waited for; matrix products, arithmetic and copies ran while one was open for 4% of the time, Pallas kernels for 0%

profile of v3, /device:TPU:1, one launch (start us, length us, event | category | flops | bytes accessed | tf_op | source)
XLA Modules:
  0.0 131.0 jit_solution(6266247887362814380)
XLA Ops:
  0.6 4.6 %collective-permute-start = (f32[4,2,64,256]{3,2,1,0:T(8,128)}, f32[4,2,64,256]{3,2,1,0:T(8,128)S(1)}, u32[]{:S(2)}, u32[]{:S(2)}) collective-permute-start(f32[4,2,64,256]{3,2,1,0:T(8,128)} %own_ref.1), channel_id=1, source_target_pairs={{1,2},{3,4},{5,6},{7,8},{9,10},{11,12},{13,14},{15,16},{17,18},{19... | collective-permute-start | bytes 1572872 | tf_op jit(solution)/shard_map/ppermute | solution.py:308
  5.2 4.9 %collective-permute-start.3 = (f32[4,2,64,256]{3,2,1,0:T(8,128)}, f32[4,2,64,256]{3,2,1,0:T(8,128)S(1)}, u32[]{:S(2)}, u32[]{:S(2)}) collective-permute-start(f32[4,2,64,256]{3,2,1,0:T(8,128)} %own_ref.1), channel_id=1, source_target_pairs={{0,1},{2,3},{4,5},{6,7},{8,9},{10,11},{12,13},{14,15},{16,17},{18,... | collective-permute-start | bytes 1572872 | tf_op jit(solution)/shard_map/ppermute | solution.py:309
  10.1 1.2 slice_bitcast_fusion.25
  11.4 0.1 broadcast_select_fusion.4
  11.5 0.7 collective-permute-start.1
  12.2 3.5 %collective-permute-start.2 = (f32[4,64,128]{2,1,0:T(8,128)S(1)}, f32[4,64,128]{2,1,0:T(8,128)S(1)}, u32[]{:S(2)}, u32[]{:S(2)}) collective-permute-start(f32[4,64,128]{2,1,0:T(8,128)S(1)} %get-tuple-element.37), channel_id=1, source_target_pairs={{0,32},{64,96},{128,160},{192,224},{256,288},{320,352},{384,416},{... | collective-permute-start | bytes 393224 | tf_op jit(solution)/shard_map/ppermute | solution.py:302
  15.7 0.0 copy-start.4
  15.7 0.1 pad_add_fusion
  15.8 0.6 copy-done.4
  16.4 0.1 pad_add_fusion.1.odd_ref
  16.5 0.0 collective-permute-done.1
  16.5 6.6 %collective-permute-done.2 = f32[4,64,128]{2,1,0:T(8,128)S(1)} collective-permute-done((f32[4,64,128]{2,1,0:T(8,128)S(1)}, f32[4,64,128]{2,1,0:T(8,128)S(1)}, u32[]{:S(2)}, u32[]{:S(2)}) %collective-permute-start.2) | collective-permute-done | bytes 131104 | tf_op jit(solution)/shard_map/ppermute | solution.py:302
  23.1 0.0 copy-start.1
  23.1 3.2 %collective-permute-start.6 = (f32[2,4,64,128]{3,2,1,0:T(8,128)S(1)}, f32[2,4,64,128]{3,2,1,0:T(8,128)S(1)}, u32[]{:S(2)}, u32[]{:S(2)}) collective-permute-start(f32[2,4,64,128]{3,2,1,0:T(8,128)S(1)} %pad_maximum_fusion.own_rims_ref), channel_id=1, source_target_pairs={{0,1},{2,3},{4,5},{6,7},{8,9},{10,11},{12,13},{14,15},{16,17},{18,... | collective-permute-start | bytes 786440 | tf_op jit(solution)/shard_map/ppermute | solution.py:312
  26.3 0.0 collective-permute-done.chip_ref
  26.3 0.1 slice_bitcast_fusion.21
  26.4 0.0 copy-start
  26.4 0.0 copy-start.2
  26.5 0.0 copy-start.3
  26.5 0.1 broadcast_select_fusion.1
  26.6 0.8 collective-permute-start.4
  27.4 10.9 %collective-permute-start.5 = (f32[4,64,128]{2,1,0:T(8,128)S(1)}, f32[4,64,128]{2,1,0:T(8,128)S(1)}, u32[]{:S(2)}, u32[]{:S(2)}) collective-permute-start(f32[4,64,128]{2,1,0:T(8,128)S(1)} %get-tuple-element.30), channel_id=1, source_target_pairs={{0,32},{64,96},{128,160},{192,224},{256,288},{320,352},{384,416},{... | collective-permute-start | bytes 393224 | tf_op jit(solution)/shard_map/ppermute | solution.py:302
  39.0 0.0 collective-permute-done.6.core_rims_ref
  39.0 0.0 collective-permute-done.3.core_ref
  39.0 0.0 collective-permute-done.4.chip_one_ref
  39.0 3.6 %collective-permute-done.5.chip_two_ref = f32[4,64,128]{2,1,0:T(8,128)S(1)} collective-permute-done((f32[4,64,128]{2,1,0:T(8,128)S(1)}, f32[4,64,128]{2,1,0:T(8,128)S(1)}, u32[]{:S(2)}, u32[]{:S(2)}) %collective-permute-start.5) | collective-permute-done | bytes 131104 | tf_op jit(solution)/shard_map/ppermute | solution.py:302
  42.6 0.0 copy-done.1
  42.6 0.0 copy-done
  42.6 0.0 copy-done.2
  42.6 0.0 copy-done.3
  42.7 7.6 %shard_map.77 = (f32[4,2,64,256]{3,2,1,0:T(8,128)S(1)}, f32[4,2,64,128]{3,2,1,0:T(8,128)S(1)}, f32[4,2,64,128]{3,2,1,0:T(8,128)S(1)}, f32[4,2,64,256]{3,2,1,0:T(...) custom-call(s32[2,2]{1,0:T(2,128)S(1)} %fusion.2.corner_ref, ...), custom_call_target="tpu_custom_call" | custom-call | tf_op jit(solution)/shard_map/pallas_call | solution.py:235
  50.2 1.4 %collective-permute-start.11 = (f32[4,2,64,128]{3,2,1,0:T(8,128)S(1)}, f32[4,2,64,128]{3,2,1,0:T(8,128)}, u32[]{:S(2)}, u32[]{:S(2)}) collective-permute-start(f32[4,2,64,128]{3,2,1,0:T(8,128)S(1)} %get-tuple-element.22), channel_id=1, source_target_pairs={{7,15},{15,23},{23,31},{8,0},{16,8},{24,16},{39,47},{47,55},{55,63... | collective-permute-start | bytes 786440 | tf_op jit(solution)/shard_map/ppermute | solution.py:342
  51.6 26.1 %all-to-all-start = ((f32[32,16,128]{2,1,0:T(8,128)}), f32[32,16,128]{2,1,0:T(8,128)S(1)}, u32[]{:S(2)}, u32[]{:S(2)}) async-start(f32[32,16,128]{2,1,0:T(8,128)} %get-tuple-element.23), calls=%async_computation | async-start | bytes 524288 | tf_op jit(solution)/shard_map/all_to_all | solution.py:276
  77.7 2.6 %collective-permute-start.7 = (f32[4,3,64,128]{3,2,1,0:T(8,128)S(1)}, f32[4,3,64,128]{3,2,1,0:T(8,128)S(1)}, u32[]{:S(2)}, u32[]{:S(2)}) collective-permute-start(f32[4,3,64,128]{3,2,1,0:T(8,128)S(1)} %get-tuple-element.18), channel_id=1, source_target_pairs={{0,32},{64,96},{128,160},{192,224},{256,288},{320,352},{384,416},{... | collective-permute-start | bytes 1179656 | tf_op jit(solution)/shard_map/ppermute | solution.py:302
  80.3 0.7 collective-permute-start.8
  81.1 0.1 pad.16.clone
  81.1 5.6 %all-to-all-done = f32[32,16,128]{2,1,0:T(8,128)S(1)} async-done(((f32[32,16,128]{2,1,0:T(8,128)}), f32[32,16,128]{2,1,0:T(8,128)S(1)}, u32[]{:S(2)}, u32[]{:S(2)}) %all-to-all-start) | async-done | bytes 262176 | tf_op jit(solution)/shard_map/all_to_all | solution.py:276
  86.8 0.7 broadcast_in_dim.7
  87.4 6.1 %all-to-all-start.1 = ((f32[16,16,128]{2,1,0:T(8,128)}), f32[16,16,128]{2,1,0:T(8,128)S(1)}, u32[]{:S(2)}, u32[]{:S(2)}) async-start(f32[16,16,128]{2,1,0:T(8,128)} %broadcast_in_dim.7), calls=%async_computation.1 | async-start | bytes 262144 | tf_op jit(solution)/shard_map/all_to_all | solution.py:276
  93.5 0.0 collective-permute-done.11
  93.6 2.2 %collective-permute-start.12 = (f32[4,2,64,128]{3,2,1,0:T(8,128)S(1)}, f32[4,2,64,128]{3,2,1,0:T(8,128)S(1)}, u32[]{:S(2)}, u32[]{:S(2)}) collective-permute-start(f32[4,2,64,128]{3,2,1,0:T(8,128)S(1)} %broadcast_select_fusion), channel_id=1, source_target_pairs={{1,2},{3,4},{5,6},{9,10},{11,12},{13,14},{17,18},{19,20},{21,22},{... | collective-permute-start | bytes 786440 | tf_op jit(solution)/shard_map/ppermute | solution.py:343
  95.7 0.0 collective-permute-done.7
  95.8 0.0 collective-permute-done.8
  95.8 0.1 select_bitcast_fusion.1
  95.9 0.1 slice_bitcast_fusion.1
  96.0 0.1 maximum_add_fusion.2
  96.2 3.4 %collective-permute-start.10 = (f32[4,2,64,128]{3,2,1,0:T(8,128)S(1)}, f32[4,2,64,128]{3,2,1,0:T(8,128)S(1)}, u32[]{:S(2)}, u32[]{:S(2)}) collective-permute-start(f32[4,2,64,128]{3,2,1,0:T(8,128)S(1)} %copy.47), channel_id=1, source_target_pairs={{1,2},{3,4},{5,6},{7,8},{9,10},{11,12},{13,14},{15,16},{17,18},{19... | collective-permute-start | bytes 786440 | tf_op jit(solution)/shard_map/ppermute | solution.py:349
  99.6 0.1 slice_bitcast_fusion.7
  99.7 0.9 maximum_add_fusion.1
  100.7 1.9 %collective-permute-start.9 = (f32[4,2,64,256]{3,2,1,0:T(8,128)}, f32[4,2,64,256]{3,2,1,0:T(8,128)S(1)}, u32[]{:S(2)}, u32[]{:S(2)}) collective-permute-start(f32[4,2,64,256]{3,2,1,0:T(8,128)} %maximum_add_fusion.1), channel_id=1, source_target_pairs={{0,1},{2,3},{4,5},{6,7},{8,9},{10,11},{12,13},{14,15},{16,17},{18,... | collective-permute-start | bytes 1572872 | tf_op jit(solution)/shard_map/ppermute | solution.py:352
  102.6 0.1 slice_bitcast_fusion.15
  102.7 0.1 slice_bitcast_fusion.13
  102.8 0.0 collective-permute-done.12
  102.8 0.1 fusion.4
  102.9 6.3 %all-to-all-done.1 = f32[16,16,128]{2,1,0:T(8,128)S(1)} async-done(((f32[16,16,128]{2,1,0:T(8,128)}), f32[16,16,128]{2,1,0:T(8,128)S(1)}, u32[]{:S(2)}, u32[]{:S(2)}) %all-to-all-start.1) | async-done | bytes 131104 | tf_op jit(solution)/shard_map/all_to_all | solution.py:276
  109.3 0.7 broadcast_in_dim.8
  109.9 11.6 %all-to-all-start.2 = ((f32[32,8,128]{2,1,0:T(8,128)}), f32[32,8,128]{2,1,0:T(8,128)S(1)}, u32[]{:S(2)}, u32[]{:S(2)}) async-start(f32[32,8,128]{2,1,0:T(8,128)} %broadcast_in_dim.8), calls=%async_computation.2 | async-start | bytes 262144 | tf_op jit(solution)/shard_map/all_to_all | solution.py:276
  121.5 0.0 collective-permute-done.10
  121.5 0.1 fusion.3
  121.7 7.6 %all-to-all-done.2 = f32[32,8,128]{2,1,0:T(8,128)S(1)} async-done(((f32[32,8,128]{2,1,0:T(8,128)}), f32[32,8,128]{2,1,0:T(8,128)S(1)}, u32[]{:S(2)}, u32[]{:S(2)}) %all-to-all-start.2) | async-done | bytes 131104 | tf_op jit(solution)/shard_map/all_to_all | solution.py:276
  129.2 0.0 collective-permute-done.9
  129.2 1.1 fusion.1
  130.4 0.7 copy.69
  (9 shorter events, 0.2 us)
Async XLA Ops:
  0.6 25.7 %collective-permute-start = (f32[4,2,64,256]{3,2,1,0:T(8,128)}, f32[4,2,64,256]{3,2,1,0:T(8,128)S(1)}, u32[]{:S(2)}, u32[]{:S(2)}) collective-permute-start(f32[4,2,64,256]{3,2,1,0:T(8,128)} %own_ref.1), channel_id=1, source_target_pairs={{1,2},{3,4},{5,6},{7,8},{9,10},{11,12},{13,14},{15,16},{17,18},{19... | collective-permute-start | bytes 1572872 | tf_op jit(solution)/shard_map/ppermute | solution.py:308
  5.2 33.8 %collective-permute-start.3 = (f32[4,2,64,256]{3,2,1,0:T(8,128)}, f32[4,2,64,256]{3,2,1,0:T(8,128)S(1)}, u32[]{:S(2)}, u32[]{:S(2)}) collective-permute-start(f32[4,2,64,256]{3,2,1,0:T(8,128)} %own_ref.1), channel_id=1, source_target_pairs={{0,1},{2,3},{4,5},{6,7},{8,9},{10,11},{12,13},{14,15},{16,17},{18,... | collective-permute-start | bytes 1572872 | tf_op jit(solution)/shard_map/ppermute | solution.py:309
  11.5 4.9 %collective-permute-start.1 = (f32[4,64,128]{2,1,0:T(8,128)S(1)}, f32[4,64,128]{2,1,0:T(8,128)S(1)}, u32[]{:S(2)}, u32[]{:S(2)}) collective-permute-start(f32[4,64,128]{2,1,0:T(8,128)S(1)} %get-tuple-element.36), channel_id=1, source_target_pairs={{32,64},{96,128},{160,192},{224,256},{288,320},{352,384},{416,448}... | collective-permute-start | bytes 393224 | tf_op jit(solution)/shard_map/ppermute | solution.py:302
  12.2 10.8 %collective-permute-start.2 = (f32[4,64,128]{2,1,0:T(8,128)S(1)}, f32[4,64,128]{2,1,0:T(8,128)S(1)}, u32[]{:S(2)}, u32[]{:S(2)}) collective-permute-start(f32[4,64,128]{2,1,0:T(8,128)S(1)} %get-tuple-element.37), channel_id=1, source_target_pairs={{0,32},{64,96},{128,160},{192,224},{256,288},{320,352},{384,416},{... | collective-permute-start | bytes 393224 | tf_op jit(solution)/shard_map/ppermute | solution.py:302
  15.7 0.7 copy-start.4
  23.1 19.6 %copy-start.1 = (bf16[2,2,2,256,256]{4,3,2,1,0:T(8,128)(2,1)S(1)}, bf16[2,2,2,256,256]{4,3,2,1,0:T(8,128)(2,1)}, u32[]{:S(2)}) copy-start(bf16[2,2,2,256,256]{4,3,2,1,0:T(8,128)(2,1)} %constant.53.clone.table_ref) | copy-start | bytes 3145732
  23.1 15.9 %collective-permute-start.6 = (f32[2,4,64,128]{3,2,1,0:T(8,128)S(1)}, f32[2,4,64,128]{3,2,1,0:T(8,128)S(1)}, u32[]{:S(2)}, u32[]{:S(2)}) collective-permute-start(f32[2,4,64,128]{3,2,1,0:T(8,128)S(1)} %pad_maximum_fusion.own_rims_ref), channel_id=1, source_target_pairs={{0,1},{2,3},{4,5},{6,7},{8,9},{10,11},{12,13},{14,15},{16,17},{18,... | collective-permute-start | bytes 786440 | tf_op jit(solution)/shard_map/ppermute | solution.py:312
  26.4 16.2 %copy-start = (f32[4,2,64,256]{3,2,1,0:T(8,128)S(1)}, f32[4,2,64,256]{3,2,1,0:T(8,128)}, u32[]{:S(2)}) copy-start(f32[4,2,64,256]{3,2,1,0:T(8,128)} %own_ref.1) | copy-start | bytes 1572868
  26.4 16.2 %copy-start.2 = (f32[2,128,128]{2,1,0:T(8,128)S(1)}, f32[2,128,128]{2,1,0:T(8,128)}, u32[]{:S(2)}) copy-start(f32[2,128,128]{2,1,0:T(8,128)} %probe_ref.1) | copy-start | bytes 393220
  26.5 16.2 %copy-start.3 = (f32[1,1,2,128,128]{4,3,2,1,0:T(8,128)S(1)}, f32[1,1,2,128,128]{4,3,2,1,0:T(8,128)}, u32[]{:S(2)}) copy-start(f32[1,1,2,128,128]{4,3,2,1,0:T(8,128)} %param.10) | copy-start | bytes 393220
  26.6 12.4 %collective-permute-start.4 = (f32[4,64,128]{2,1,0:T(8,128)S(1)}, f32[4,64,128]{2,1,0:T(8,128)S(1)}, u32[]{:S(2)}, u32[]{:S(2)}) collective-permute-start(f32[4,64,128]{2,1,0:T(8,128)S(1)} %get-tuple-element.31), channel_id=1, source_target_pairs={{32,64},{96,128},{160,192},{224,256},{288,320},{352,384},{416,448}... | collective-permute-start | bytes 393224 | tf_op jit(solution)/shard_map/ppermute | solution.py:302
  27.4 15.2 %collective-permute-start.5 = (f32[4,64,128]{2,1,0:T(8,128)S(1)}, f32[4,64,128]{2,1,0:T(8,128)S(1)}, u32[]{:S(2)}, u32[]{:S(2)}) collective-permute-start(f32[4,64,128]{2,1,0:T(8,128)S(1)} %get-tuple-element.30), channel_id=1, source_target_pairs={{0,32},{64,96},{128,160},{192,224},{256,288},{320,352},{384,416},{... | collective-permute-start | bytes 393224 | tf_op jit(solution)/shard_map/ppermute | solution.py:302
  50.2 43.3 %collective-permute-start.11 = (f32[4,2,64,128]{3,2,1,0:T(8,128)S(1)}, f32[4,2,64,128]{3,2,1,0:T(8,128)}, u32[]{:S(2)}, u32[]{:S(2)}) collective-permute-start(f32[4,2,64,128]{3,2,1,0:T(8,128)S(1)} %get-tuple-element.22), channel_id=1, source_target_pairs={{7,15},{15,23},{23,31},{8,0},{16,8},{24,16},{39,47},{47,55},{55,63... | collective-permute-start | bytes 786440 | tf_op jit(solution)/shard_map/ppermute | solution.py:342
  51.6 35.1 %all-to-all-start = ((f32[32,16,128]{2,1,0:T(8,128)}), f32[32,16,128]{2,1,0:T(8,128)S(1)}, u32[]{:S(2)}, u32[]{:S(2)}) async-start(f32[32,16,128]{2,1,0:T(8,128)} %get-tuple-element.23), calls=%async_computation | async-start | bytes 524288 | tf_op jit(solution)/shard_map/all_to_all | solution.py:276
  77.7 18.0 %collective-permute-start.7 = (f32[4,3,64,128]{3,2,1,0:T(8,128)S(1)}, f32[4,3,64,128]{3,2,1,0:T(8,128)S(1)}, u32[]{:S(2)}, u32[]{:S(2)}) collective-permute-start(f32[4,3,64,128]{3,2,1,0:T(8,128)S(1)} %get-tuple-element.18), channel_id=1, source_target_pairs={{0,32},{64,96},{128,160},{192,224},{256,288},{320,352},{384,416},{... | collective-permute-start | bytes 1179656 | tf_op jit(solution)/shard_map/ppermute | solution.py:302
  80.3 15.4 %collective-permute-start.8 = (f32[4,3,64,128]{3,2,1,0:T(8,128)S(1)}, f32[4,3,64,128]{3,2,1,0:T(8,128)S(1)}, u32[]{:S(2)}, u32[]{:S(2)}) collective-permute-start(f32[4,3,64,128]{3,2,1,0:T(8,128)S(1)} %get-tuple-element.19), channel_id=1, source_target_pairs={{32,64},{96,128},{160,192},{224,256},{288,320},{352,384},{416,448}... | collective-permute-start | bytes 1179656 | tf_op jit(solution)/shard_map/ppermute | solution.py:302
  87.4 21.8 %all-to-all-start.1 = ((f32[16,16,128]{2,1,0:T(8,128)}), f32[16,16,128]{2,1,0:T(8,128)S(1)}, u32[]{:S(2)}, u32[]{:S(2)}) async-start(f32[16,16,128]{2,1,0:T(8,128)} %broadcast_in_dim.7), calls=%async_computation.1 | async-start | bytes 262144 | tf_op jit(solution)/shard_map/all_to_all | solution.py:276
  93.6 9.2 %collective-permute-start.12 = (f32[4,2,64,128]{3,2,1,0:T(8,128)S(1)}, f32[4,2,64,128]{3,2,1,0:T(8,128)S(1)}, u32[]{:S(2)}, u32[]{:S(2)}) collective-permute-start(f32[4,2,64,128]{3,2,1,0:T(8,128)S(1)} %broadcast_select_fusion), channel_id=1, source_target_pairs={{1,2},{3,4},{5,6},{9,10},{11,12},{13,14},{17,18},{19,20},{21,22},{... | collective-permute-start | bytes 786440 | tf_op jit(solution)/shard_map/ppermute | solution.py:343
  96.2 25.4 %collective-permute-start.10 = (f32[4,2,64,128]{3,2,1,0:T(8,128)S(1)}, f32[4,2,64,128]{3,2,1,0:T(8,128)S(1)}, u32[]{:S(2)}, u32[]{:S(2)}) collective-permute-start(f32[4,2,64,128]{3,2,1,0:T(8,128)S(1)} %copy.47), channel_id=1, source_target_pairs={{1,2},{3,4},{5,6},{7,8},{9,10},{11,12},{13,14},{15,16},{17,18},{19... | collective-permute-start | bytes 786440 | tf_op jit(solution)/shard_map/ppermute | solution.py:349
  100.7 28.6 %collective-permute-start.9 = (f32[4,2,64,256]{3,2,1,0:T(8,128)}, f32[4,2,64,256]{3,2,1,0:T(8,128)S(1)}, u32[]{:S(2)}, u32[]{:S(2)}) collective-permute-start(f32[4,2,64,256]{3,2,1,0:T(8,128)} %maximum_add_fusion.1), channel_id=1, source_target_pairs={{0,1},{2,3},{4,5},{6,7},{8,9},{10,11},{12,13},{14,15},{16,17},{18,... | collective-permute-start | bytes 1572872 | tf_op jit(solution)/shard_map/ppermute | solution.py:352
  109.9 19.3 %all-to-all-start.2 = ((f32[32,8,128]{2,1,0:T(8,128)}), f32[32,8,128]{2,1,0:T(8,128)S(1)}, u32[]{:S(2)}, u32[]{:S(2)}) async-start(f32[32,8,128]{2,1,0:T(8,128)} %broadcast_in_dim.8), calls=%async_computation.2 | async-start | bytes 262144 | tf_op jit(solution)/shard_map/all_to_all | solution.py:276

commit v4 on v3

--- a/solution.py
+++ b/solution.py
@@ -116,7 +116,7 @@
     core_row = pl.multiple_of((1 - odd_ref[0]) * 2 * HALF, HALF)
     bands = (pl.ds(chip_row, HALF), slice(HALF, 2 * HALF), pl.ds(core_row, HALF))
     odd_column = odd_ref[1] == 1
-    for s in range(SLICES):
+    def assemble(s):
         for c in range(2):
             for b, band_ref in enumerate((chip_ref, own_ref, core_ref)):
                 extended[s, c, 1, bands[b], :] = band_ref[s, c, :, :SIDE]
@@ -139,11 +139,12 @@
     for k in range(SLOTS):
         row, col = corner_ref[k, 0], corner_ref[k, 1] + HALF
         places.append((row, col // SIDE, col % SIDE))
-    for k in range(SLOTS):
-        row, block, shift = places[k]
-        back = (SIDE - shift) % SIDE
-        inside = lanes < SIDE - shift
-        for s in range(SLICES):
+    def extract(s):
+        assemble(s)
+        for k in range(SLOTS):
+            row, block, shift = places[k]
+            back = (SIDE - shift) % SIDE
+            inside = lanes < SIDE - shift
             for c in range(2):
                 near = extended[s, c, block, pl.ds(row, SIDE), :]
                 far = extended[s, c, block + 1, pl.ds(row, SIDE), :]
@@ -155,9 +156,11 @@
         return (windows[k, s, 0], windows[k, s, 1])
 
     slots = range(SLOTS)
+    extract(0)
     fields = [times(probe, layer(k, 0)) for k in slots]
     for s in range(1, SLICES):
         arrived = two_sided(fields, table_ref, 0, False)
+        extract(s)
         for k in slots:
             waves[k, s - 1, 0] = arrived[k][0]
             waves[k, s - 1, 1] = arrived[k][1]
@@ -180,19 +183,7 @@
             total[s, c, block, pl.ds(row, SIDE), :] += jnp.where(inside, moved, 0.0)
             total[s, c, block + 1, pl.ds(row, SIDE), :] += jnp.where(inside, 0.0, moved)
 
-    for s in range(SLICES - 1, 0, -1):
-        for k in slots:
-            add(k, s, conj_times((waves[k, s - 1, 0], waves[k, s - 1, 1]), backward[k]))
-        backward = two_sided([conj_times(layer(k, s), backward[k]) for k in slots], table_ref, 0, True)
-    for k in slots:
-        add(k, 0, conj_times(probe, backward[k]))
-    terms = [conj_times(layer(k, 0), backward[k]) for k in slots]
-    for c in range(2):
-        summed = (terms[0][c] + terms[1][c]).reshape(16, 8, SIDE)
-        payload_out[c * 16 : (c + 1) * 16, 0:8, :] = summed
-    payload_out[:, 8:16, :] = jnp.full((32, 8, SIDE), count_ref[0].astype(jnp.float32), jnp.float32)
-
-    for s in range(SLICES):
+    def emit(s):
         for c in range(2):
             first, second = total[s, c, 1, bands[0], :], total[s, c, 2, bands[0], :]
             edge_out[s, c] = jnp.where(low_lanes, first, second)
@@ -210,6 +201,20 @@
             one_out[s, b] = jnp.where(odd_column, right, left)
             two_out[s, b] = jnp.where(odd_column, left, right)
 
+    for s in range(SLICES - 1, 0, -1):
+        for k in slots:
+            add(k, s, conj_times((waves[k, s - 1, 0], waves[k, s - 1, 1]), backward[k]))
+        backward = two_sided([conj_times(layer(k, s), backward[k]) for k in slots], table_ref, 0, True)
+        emit(s)
+    for k in slots:
+        add(k, 0, conj_times(probe, backward[k]))
+    emit(0)
+    terms = [conj_times(layer(k, 0), backward[k]) for k in slots]
+    for c in range(2):
+        summed = (terms[0][c] + terms[1][c]).reshape(16, 8, SIDE)
+        payload_out[c * 16 : (c + 1) * 16, 0:8, :] = summed
+    payload_out[:, 8:16, :] = jnp.full((32, 8, SIDE), count_ref[0].astype(jnp.float32), jnp.float32)
+
 
 def gradients(*operands):
     f32 = jnp.float32

time: 132 us -> 131 us (level)
  no operation moved by 1% of the time
where the time goes in v4:
time: 131 us
  starting transfers between devices  84.5 us (65%)
  waiting for transfers between devices  29.7 us (23%)
  Pallas kernels  7.25 us (6%)
  local copies, waits for them, and re-layouts  4.79 us (4%)
  other arithmetic  2.87 us (2%)
  between operations  1.7 us (1%)
    all_to_all x3, starting transfers between devices, exchange(): lax.all_to_all(pieces, ('gx', 'gy'), 0, 0, tiled=True, axis_index_groups=...  43.8 us
    all_to_all x3, waiting for transfers between devices, exchange(): lax.all_to_all(pieces, ('gx', 'gy'), 0, 0, tiled=True, axis_index_groups=...  19.4 us
    ppermute x6, starting transfers between devices, swap(): return (lax.ppermute(first, 'gx', ones), lax.ppermute(second, 'gx', twos))  19.1 us
    ppermute x6, waiting for transfers between devices, swap(): return (lax.ppermute(first, 'gx', ones), lax.ppermute(second, 'gx', twos))  10.2 us
    pallas_call x1, Pallas kernels, gradients(): pl.pallas_call(patch_kernel, grid=(1,), out_shape=shapes, in_specs=[smem]...  7.25 us
    ppermute x1, starting transfers between devices, body(): core_band = plain(lax.ppermute(plain(object_slices), 'gy', cores))  4.89 us
    ppermute x1, starting transfers between devices, body(): chip_band = plain(lax.ppermute(plain(object_slices), 'gy', chips))  4.6 us
    ppermute x1, starting transfers between devices, body(): edge = plain(lax.ppermute(plain(edge), 'gy', chips))  3.39 us
  transfers between devices with their start and end apart: 16, of which 5 were waited for; matrix products, arithmetic and copies ran while one was open for 4% of the time, Pallas kernels for 0%

profile of v4, /device:TPU:1, one launch (start us, length us, event | category | flops | bytes accessed | tf_op | source)
XLA Modules:
  0.0 130.7 jit_solution(17027973892915090295)
XLA Ops:
  0.6 4.6 %collective-permute-start = (f32[4,2,64,256]{3,2,1,0:T(8,128)}, f32[4,2,64,256]{3,2,1,0:T(8,128)S(1)}, u32[]{:S(2)}, u32[]{:S(2)}) collective-permute-start(f32[4,2,64,256]{3,2,1,0:T(8,128)} %own_ref.1), channel_id=1, source_target_pairs={{1,2},{3,4},{5,6},{7,8},{9,10},{11,12},{13,14},{15,16},{17,18},{19... | collective-permute-start | bytes 1572872 | tf_op jit(solution)/shard_map/ppermute | solution.py:313
  5.2 4.9 %collective-permute-start.3 = (f32[4,2,64,256]{3,2,1,0:T(8,128)}, f32[4,2,64,256]{3,2,1,0:T(8,128)S(1)}, u32[]{:S(2)}, u32[]{:S(2)}) collective-permute-start(f32[4,2,64,256]{3,2,1,0:T(8,128)} %own_ref.1), channel_id=1, source_target_pairs={{0,1},{2,3},{4,5},{6,7},{8,9},{10,11},{12,13},{14,15},{16,17},{18,... | collective-permute-start | bytes 1572872 | tf_op jit(solution)/shard_map/ppermute | solution.py:314
  10.1 1.2 slice_bitcast_fusion.25
  11.4 0.1 broadcast_select_fusion.4
  11.5 0.7 collective-permute-start.1
  12.2 3.5 %collective-permute-start.2 = (f32[4,64,128]{2,1,0:T(8,128)S(1)}, f32[4,64,128]{2,1,0:T(8,128)S(1)}, u32[]{:S(2)}, u32[]{:S(2)}) collective-permute-start(f32[4,64,128]{2,1,0:T(8,128)S(1)} %get-tuple-element.37), channel_id=1, source_target_pairs={{0,32},{64,96},{128,160},{192,224},{256,288},{320,352},{384,416},{... | collective-permute-start | bytes 393224 | tf_op jit(solution)/shard_map/ppermute | solution.py:307
  15.7 0.0 copy-start.4
  15.7 0.1 pad_add_fusion
  15.8 0.6 copy-done.4
  16.4 0.1 pad_add_fusion.1.odd_ref
  16.5 0.0 collective-permute-done.1
  16.5 6.6 %collective-permute-done.2 = f32[4,64,128]{2,1,0:T(8,128)S(1)} collective-permute-done((f32[4,64,128]{2,1,0:T(8,128)S(1)}, f32[4,64,128]{2,1,0:T(8,128)S(1)}, u32[]{:S(2)}, u32[]{:S(2)}) %collective-permute-start.2) | collective-permute-done | bytes 131104 | tf_op jit(solution)/shard_map/ppermute | solution.py:307
  23.1 0.0 copy-start.1
  23.1 3.2 %collective-permute-start.6 = (f32[2,4,64,128]{3,2,1,0:T(8,128)S(1)}, f32[2,4,64,128]{3,2,1,0:T(8,128)S(1)}, u32[]{:S(2)}, u32[]{:S(2)}) collective-permute-start(f32[2,4,64,128]{3,2,1,0:T(8,128)S(1)} %pad_maximum_fusion.own_rims_ref), channel_id=1, source_target_pairs={{0,1},{2,3},{4,5},{6,7},{8,9},{10,11},{12,13},{14,15},{16,17},{18,... | collective-permute-start | bytes 786440 | tf_op jit(solution)/shard_map/ppermute | solution.py:317
  26.3 0.0 collective-permute-done.chip_ref
  26.3 0.1 slice_bitcast_fusion.21
  26.4 0.0 copy-start
  26.4 0.0 copy-start.2
  26.5 0.0 copy-start.3
  26.5 0.1 broadcast_select_fusion.1
  26.6 0.8 collective-permute-start.4
  27.4 10.9 %collective-permute-start.5 = (f32[4,64,128]{2,1,0:T(8,128)S(1)}, f32[4,64,128]{2,1,0:T(8,128)S(1)}, u32[]{:S(2)}, u32[]{:S(2)}) collective-permute-start(f32[4,64,128]{2,1,0:T(8,128)S(1)} %get-tuple-element.30), channel_id=1, source_target_pairs={{0,32},{64,96},{128,160},{192,224},{256,288},{320,352},{384,416},{... | collective-permute-start | bytes 393224 | tf_op jit(solution)/shard_map/ppermute | solution.py:307
  39.0 0.0 collective-permute-done.6.core_rims_ref
  39.0 0.0 collective-permute-done.3.core_ref
  39.0 0.0 collective-permute-done.4.chip_one_ref
  39.0 3.6 %collective-permute-done.5.chip_two_ref = f32[4,64,128]{2,1,0:T(8,128)S(1)} collective-permute-done((f32[4,64,128]{2,1,0:T(8,128)S(1)}, f32[4,64,128]{2,1,0:T(8,128)S(1)}, u32[]{:S(2)}, u32[]{:S(2)}) %collective-permute-start.5) | collective-permute-done | bytes 131104 | tf_op jit(solution)/shard_map/ppermute | solution.py:307
  42.6 0.0 copy-done.1
  42.6 0.0 copy-done
  42.6 0.0 copy-done.2
  42.6 0.0 copy-done.3
  42.7 7.2 %shard_map.77 = (f32[4,2,64,256]{3,2,1,0:T(8,128)S(1)}, f32[4,2,64,128]{3,2,1,0:T(8,128)S(1)}, f32[4,2,64,128]{3,2,1,0:T(8,128)S(1)}, f32[4,2,64,256]{3,2,1,0:T(...) custom-call(s32[2,2]{1,0:T(2,128)S(1)} %fusion.2.corner_ref, ...), custom_call_target="tpu_custom_call" | custom-call | tf_op jit(solution)/shard_map/pallas_call | solution.py:240
  49.9 1.4 %collective-permute-start.11 = (f32[4,2,64,128]{3,2,1,0:T(8,128)S(1)}, f32[4,2,64,128]{3,2,1,0:T(8,128)}, u32[]{:S(2)}, u32[]{:S(2)}) collective-permute-start(f32[4,2,64,128]{3,2,1,0:T(8,128)S(1)} %get-tuple-element.22), channel_id=1, source_target_pairs={{7,15},{15,23},{23,31},{8,0},{16,8},{24,16},{39,47},{47,55},{55,63... | collective-permute-start | bytes 786440 | tf_op jit(solution)/shard_map/ppermute | solution.py:347
  51.3 26.1 %all-to-all-start = ((f32[32,16,128]{2,1,0:T(8,128)}), f32[32,16,128]{2,1,0:T(8,128)S(1)}, u32[]{:S(2)}, u32[]{:S(2)}) async-start(f32[32,16,128]{2,1,0:T(8,128)} %get-tuple-element.23), calls=%async_computation | async-start | bytes 524288 | tf_op jit(solution)/shard_map/all_to_all | solution.py:281
  77.4 2.6 %collective-permute-start.7 = (f32[4,3,64,128]{3,2,1,0:T(8,128)S(1)}, f32[4,3,64,128]{3,2,1,0:T(8,128)S(1)}, u32[]{:S(2)}, u32[]{:S(2)}) collective-permute-start(f32[4,3,64,128]{3,2,1,0:T(8,128)S(1)} %get-tuple-element.18), channel_id=1, source_target_pairs={{0,32},{64,96},{128,160},{192,224},{256,288},{320,352},{384,416},{... | collective-permute-start | bytes 1179656 | tf_op jit(solution)/shard_map/ppermute | solution.py:307
  80.0 0.7 collective-permute-start.8
  80.7 0.1 pad.16.clone
  80.8 5.6 %all-to-all-done = f32[32,16,128]{2,1,0:T(8,128)S(1)} async-done(((f32[32,16,128]{2,1,0:T(8,128)}), f32[32,16,128]{2,1,0:T(8,128)S(1)}, u32[]{:S(2)}, u32[]{:S(2)}) %all-to-all-start) | async-done | bytes 262176 | tf_op jit(solution)/shard_map/all_to_all | solution.py:281
  86.4 0.7 broadcast_in_dim.7
  87.1 6.1 %all-to-all-start.1 = ((f32[16,16,128]{2,1,0:T(8,128)}), f32[16,16,128]{2,1,0:T(8,128)S(1)}, u32[]{:S(2)}, u32[]{:S(2)}) async-start(f32[16,16,128]{2,1,0:T(8,128)} %broadcast_in_dim.7), calls=%async_computation.1 | async-start | bytes 262144 | tf_op jit(solution)/shard_map/all_to_all | solution.py:281
  93.2 0.0 collective-permute-done.11
  93.2 2.2 %collective-permute-start.12 = (f32[4,2,64,128]{3,2,1,0:T(8,128)S(1)}, f32[4,2,64,128]{3,2,1,0:T(8,128)S(1)}, u32[]{:S(2)}, u32[]{:S(2)}) collective-permute-start(f32[4,2,64,128]{3,2,1,0:T(8,128)S(1)} %broadcast_select_fusion), channel_id=1, source_target_pairs={{1,2},{3,4},{5,6},{9,10},{11,12},{13,14},{17,18},{19,20},{21,22},{... | collective-permute-start | bytes 786440 | tf_op jit(solution)/shard_map/ppermute | solution.py:348
  95.4 0.0 collective-permute-done.7
  95.4 0.0 collective-permute-done.8
  95.4 0.1 select_bitcast_fusion.1
  95.5 0.1 slice_bitcast_fusion.1
  95.7 0.1 maximum_add_fusion.2
  95.8 3.4 %collective-permute-start.10 = (f32[4,2,64,128]{3,2,1,0:T(8,128)S(1)}, f32[4,2,64,128]{3,2,1,0:T(8,128)S(1)}, u32[]{:S(2)}, u32[]{:S(2)}) collective-permute-start(f32[4,2,64,128]{3,2,1,0:T(8,128)S(1)} %copy.47), channel_id=1, source_target_pairs={{1,2},{3,4},{5,6},{7,8},{9,10},{11,12},{13,14},{15,16},{17,18},{19... | collective-permute-start | bytes 786440 | tf_op jit(solution)/shard_map/ppermute | solution.py:354
  99.2 0.1 slice_bitcast_fusion.7
  99.4 0.9 maximum_add_fusion.1
  100.3 1.9 %collective-permute-start.9 = (f32[4,2,64,256]{3,2,1,0:T(8,128)}, f32[4,2,64,256]{3,2,1,0:T(8,128)S(1)}, u32[]{:S(2)}, u32[]{:S(2)}) collective-permute-start(f32[4,2,64,256]{3,2,1,0:T(8,128)} %maximum_add_fusion.1), channel_id=1, source_target_pairs={{0,1},{2,3},{4,5},{6,7},{8,9},{10,11},{12,13},{14,15},{16,17},{18,... | collective-permute-start | bytes 1572872 | tf_op jit(solution)/shard_map/ppermute | solution.py:357
  102.3 0.1 slice_bitcast_fusion.15
  102.4 0.1 slice_bitcast_fusion.13
  102.5 0.0 collective-permute-done.12
  102.5 0.1 fusion.4
  102.6 6.3 %all-to-all-done.1 = f32[16,16,128]{2,1,0:T(8,128)S(1)} async-done(((f32[16,16,128]{2,1,0:T(8,128)}), f32[16,16,128]{2,1,0:T(8,128)S(1)}, u32[]{:S(2)}, u32[]{:S(2)}) %all-to-all-start.1) | async-done | bytes 131104 | tf_op jit(solution)/shard_map/all_to_all | solution.py:281
  108.9 0.7 broadcast_in_dim.8
  109.6 11.6 %all-to-all-start.2 = ((f32[32,8,128]{2,1,0:T(8,128)}), f32[32,8,128]{2,1,0:T(8,128)S(1)}, u32[]{:S(2)}, u32[]{:S(2)}) async-start(f32[32,8,128]{2,1,0:T(8,128)} %broadcast_in_dim.8), calls=%async_computation.2 | async-start | bytes 262144 | tf_op jit(solution)/shard_map/all_to_all | solution.py:281
  121.2 0.0 collective-permute-done.10
  121.2 0.1 fusion.3
  121.4 7.6 %all-to-all-done.2 = f32[32,8,128]{2,1,0:T(8,128)S(1)} async-done(((f32[32,8,128]{2,1,0:T(8,128)}), f32[32,8,128]{2,1,0:T(8,128)S(1)}, u32[]{:S(2)}, u32[]{:S(2)}) %all-to-all-start.2) | async-done | bytes 131104 | tf_op jit(solution)/shard_map/all_to_all | solution.py:281
  128.9 0.0 collective-permute-done.9
  128.9 1.1 fusion.1
  130.1 0.7 copy.69
  (9 shorter events, 0.2 us)
Async XLA Ops:
  0.6 25.7 %collective-permute-start = (f32[4,2,64,256]{3,2,1,0:T(8,128)}, f32[4,2,64,256]{3,2,1,0:T(8,128)S(1)}, u32[]{:S(2)}, u32[]{:S(2)}) collective-permute-start(f32[4,2,64,256]{3,2,1,0:T(8,128)} %own_ref.1), channel_id=1, source_target_pairs={{1,2},{3,4},{5,6},{7,8},{9,10},{11,12},{13,14},{15,16},{17,18},{19... | collective-permute-start | bytes 1572872 | tf_op jit(solution)/shard_map/ppermute | solution.py:313
  5.2 33.8 %collective-permute-start.3 = (f32[4,2,64,256]{3,2,1,0:T(8,128)}, f32[4,2,64,256]{3,2,1,0:T(8,128)S(1)}, u32[]{:S(2)}, u32[]{:S(2)}) collective-permute-start(f32[4,2,64,256]{3,2,1,0:T(8,128)} %own_ref.1), channel_id=1, source_target_pairs={{0,1},{2,3},{4,5},{6,7},{8,9},{10,11},{12,13},{14,15},{16,17},{18,... | collective-permute-start | bytes 1572872 | tf_op jit(solution)/shard_map/ppermute | solution.py:314
  11.5 4.9 %collective-permute-start.1 = (f32[4,64,128]{2,1,0:T(8,128)S(1)}, f32[4,64,128]{2,1,0:T(8,128)S(1)}, u32[]{:S(2)}, u32[]{:S(2)}) collective-permute-start(f32[4,64,128]{2,1,0:T(8,128)S(1)} %get-tuple-element.36), channel_id=1, source_target_pairs={{32,64},{96,128},{160,192},{224,256},{288,320},{352,384},{416,448}... | collective-permute-start | bytes 393224 | tf_op jit(solution)/shard_map/ppermute | solution.py:307
  12.2 10.8 %collective-permute-start.2 = (f32[4,64,128]{2,1,0:T(8,128)S(1)}, f32[4,64,128]{2,1,0:T(8,128)S(1)}, u32[]{:S(2)}, u32[]{:S(2)}) collective-permute-start(f32[4,64,128]{2,1,0:T(8,128)S(1)} %get-tuple-element.37), channel_id=1, source_target_pairs={{0,32},{64,96},{128,160},{192,224},{256,288},{320,352},{384,416},{... | collective-permute-start | bytes 393224 | tf_op jit(solution)/shard_map/ppermute | solution.py:307
  15.7 0.7 copy-start.4
  23.1 19.6 %copy-start.1 = (bf16[2,2,2,256,256]{4,3,2,1,0:T(8,128)(2,1)S(1)}, bf16[2,2,2,256,256]{4,3,2,1,0:T(8,128)(2,1)}, u32[]{:S(2)}) copy-start(bf16[2,2,2,256,256]{4,3,2,1,0:T(8,128)(2,1)} %constant.53.clone.table_ref) | copy-start | bytes 3145732
  23.1 15.9 %collective-permute-start.6 = (f32[2,4,64,128]{3,2,1,0:T(8,128)S(1)}, f32[2,4,64,128]{3,2,1,0:T(8,128)S(1)}, u32[]{:S(2)}, u32[]{:S(2)}) collective-permute-start(f32[2,4,64,128]{3,2,1,0:T(8,128)S(1)} %pad_maximum_fusion.own_rims_ref), channel_id=1, source_target_pairs={{0,1},{2,3},{4,5},{6,7},{8,9},{10,11},{12,13},{14,15},{16,17},{18,... | collective-permute-start | bytes 786440 | tf_op jit(solution)/shard_map/ppermute | solution.py:317
  26.4 16.2 %copy-start = (f32[4,2,64,256]{3,2,1,0:T(8,128)S(1)}, f32[4,2,64,256]{3,2,1,0:T(8,128)}, u32[]{:S(2)}) copy-start(f32[4,2,64,256]{3,2,1,0:T(8,128)} %own_ref.1) | copy-start | bytes 1572868
  26.4 16.2 %copy-start.2 = (f32[2,128,128]{2,1,0:T(8,128)S(1)}, f32[2,128,128]{2,1,0:T(8,128)}, u32[]{:S(2)}) copy-start(f32[2,128,128]{2,1,0:T(8,128)} %probe_ref.1) | copy-start | bytes 393220
  26.5 16.2 %copy-start.3 = (f32[1,1,2,128,128]{4,3,2,1,0:T(8,128)S(1)}, f32[1,1,2,128,128]{4,3,2,1,0:T(8,128)}, u32[]{:S(2)}) copy-start(f32[1,1,2,128,128]{4,3,2,1,0:T(8,128)} %param.10) | copy-start | bytes 393220
  26.6 12.4 %collective-permute-start.4 = (f32[4,64,128]{2,1,0:T(8,128)S(1)}, f32[4,64,128]{2,1,0:T(8,128)S(1)}, u32[]{:S(2)}, u32[]{:S(2)}) collective-permute-start(f32[4,64,128]{2,1,0:T(8,128)S(1)} %get-tuple-element.31), channel_id=1, source_target_pairs={{32,64},{96,128},{160,192},{224,256},{288,320},{352,384},{416,448}... | collective-permute-start | bytes 393224 | tf_op jit(solution)/shard_map/ppermute | solution.py:307
  27.4 15.2 %collective-permute-start.5 = (f32[4,64,128]{2,1,0:T(8,128)S(1)}, f32[4,64,128]{2,1,0:T(8,128)S(1)}, u32[]{:S(2)}, u32[]{:S(2)}) collective-permute-start(f32[4,64,128]{2,1,0:T(8,128)S(1)} %get-tuple-element.30), channel_id=1, source_target_pairs={{0,32},{64,96},{128,160},{192,224},{256,288},{320,352},{384,416},{... | collective-permute-start | bytes 393224 | tf_op jit(solution)/shard_map/ppermute | solution.py:307
  49.9 43.3 %collective-permute-start.11 = (f32[4,2,64,128]{3,2,1,0:T(8,128)S(1)}, f32[4,2,64,128]{3,2,1,0:T(8,128)}, u32[]{:S(2)}, u32[]{:S(2)}) collective-permute-start(f32[4,2,64,128]{3,2,1,0:T(8,128)S(1)} %get-tuple-element.22), channel_id=1, source_target_pairs={{7,15},{15,23},{23,31},{8,0},{16,8},{24,16},{39,47},{47,55},{55,63... | collective-permute-start | bytes 786440 | tf_op jit(solution)/shard_map/ppermute | solution.py:347
  51.3 35.1 %all-to-all-start = ((f32[32,16,128]{2,1,0:T(8,128)}), f32[32,16,128]{2,1,0:T(8,128)S(1)}, u32[]{:S(2)}, u32[]{:S(2)}) async-start(f32[32,16,128]{2,1,0:T(8,128)} %get-tuple-element.23), calls=%async_computation | async-start | bytes 524288 | tf_op jit(solution)/shard_map/all_to_all | solution.py:281
  77.4 18.0 %collective-permute-start.7 = (f32[4,3,64,128]{3,2,1,0:T(8,128)S(1)}, f32[4,3,64,128]{3,2,1,0:T(8,128)S(1)}, u32[]{:S(2)}, u32[]{:S(2)}) collective-permute-start(f32[4,3,64,128]{3,2,1,0:T(8,128)S(1)} %get-tuple-element.18), channel_id=1, source_target_pairs={{0,32},{64,96},{128,160},{192,224},{256,288},{320,352},{384,416},{... | collective-permute-start | bytes 1179656 | tf_op jit(solution)/shard_map/ppermute | solution.py:307
  80.0 15.4 %collective-permute-start.8 = (f32[4,3,64,128]{3,2,1,0:T(8,128)S(1)}, f32[4,3,64,128]{3,2,1,0:T(8,128)S(1)}, u32[]{:S(2)}, u32[]{:S(2)}) collective-permute-start(f32[4,3,64,128]{3,2,1,0:T(8,128)S(1)} %get-tuple-element.19), channel_id=1, source_target_pairs={{32,64},{96,128},{160,192},{224,256},{288,320},{352,384},{416,448}... | collective-permute-start | bytes 1179656 | tf_op jit(solution)/shard_map/ppermute | solution.py:307
  87.1 21.8 %all-to-all-start.1 = ((f32[16,16,128]{2,1,0:T(8,128)}), f32[16,16,128]{2,1,0:T(8,128)S(1)}, u32[]{:S(2)}, u32[]{:S(2)}) async-start(f32[16,16,128]{2,1,0:T(8,128)} %broadcast_in_dim.7), calls=%async_computation.1 | async-start | bytes 262144 | tf_op jit(solution)/shard_map/all_to_all | solution.py:281
  93.2 9.2 %collective-permute-start.12 = (f32[4,2,64,128]{3,2,1,0:T(8,128)S(1)}, f32[4,2,64,128]{3,2,1,0:T(8,128)S(1)}, u32[]{:S(2)}, u32[]{:S(2)}) collective-permute-start(f32[4,2,64,128]{3,2,1,0:T(8,128)S(1)} %broadcast_select_fusion), channel_id=1, source_target_pairs={{1,2},{3,4},{5,6},{9,10},{11,12},{13,14},{17,18},{19,20},{21,22},{... | collective-permute-start | bytes 786440 | tf_op jit(solution)/shard_map/ppermute | solution.py:348
  95.8 25.4 %collective-permute-start.10 = (f32[4,2,64,128]{3,2,1,0:T(8,128)S(1)}, f32[4,2,64,128]{3,2,1,0:T(8,128)S(1)}, u32[]{:S(2)}, u32[]{:S(2)}) collective-permute-start(f32[4,2,64,128]{3,2,1,0:T(8,128)S(1)} %copy.47), channel_id=1, source_target_pairs={{1,2},{3,4},{5,6},{7,8},{9,10},{11,12},{13,14},{15,16},{17,18},{19... | collective-permute-start | bytes 786440 | tf_op jit(solution)/shard_map/ppermute | solution.py:354
  100.3 28.6 %collective-permute-start.9 = (f32[4,2,64,256]{3,2,1,0:T(8,128)}, f32[4,2,64,256]{3,2,1,0:T(8,128)S(1)}, u32[]{:S(2)}, u32[]{:S(2)}) collective-permute-start(f32[4,2,64,256]{3,2,1,0:T(8,128)} %maximum_add_fusion.1), channel_id=1, source_target_pairs={{0,1},{2,3},{4,5},{6,7},{8,9},{10,11},{12,13},{14,15},{16,17},{18,... | collective-permute-start | bytes 1572872 | tf_op jit(solution)/shard_map/ppermute | solution.py:357
  109.6 19.3 %all-to-all-start.2 = ((f32[32,8,128]{2,1,0:T(8,128)}), f32[32,8,128]{2,1,0:T(8,128)S(1)}, u32[]{:S(2)}, u32[]{:S(2)}) async-start(f32[32,8,128]{2,1,0:T(8,128)} %broadcast_in_dim.8), calls=%async_computation.2 | async-start | bytes 262144 | tf_op jit(solution)/shard_map/all_to_all | solution.py:281
